TPU v7x, 128 devices: a whole 4x4x4 slice. The times are simulated.
128 devices in a mesh: pipe: 4 (over x_lo, core), tensor: 8 (over z, x_hi), dp: 4 (over y).
Axes of the slice: x: 4 (x_hi: 2, x_lo: 2; x = x_hi * 2 + x_lo), y: 4, z: 4, core: 2. Of those that a mesh axis runs over, the one named last changes fastest.
Arguments:
- cotangent: bfloat16 [8, 192, 4096], P('dp', 'tensor'), may hold values from -6 to 6
- saved_u: bfloat16 [4, 8, 192, 12288], P('pipe', 'dp', None, 'tensor'), may hold values from -3 to 3
- dt_raw: float32 [4, 8, 192, 128], P('pipe', 'dp', None, 'tensor'), may hold values from -5 to 5
- in_weight: bfloat16 [4, 4096, 12288], P('pipe', None, 'tensor'), may hold values from -0.0390625 to 0.0390625
- out_weight: bfloat16 [4, 8192, 4096], P('pipe', 'tensor'), may hold values from -0.0625 to 0.0625
- conv_weight: float32 [4, 4, 12288], P('pipe', None, 'tensor'), may hold values from -3 to 3
- conv_bias: float32 [4, 12288], P('pipe', 'tensor'), may hold values from -3 to 3
- a_log: float32 [4, 128], P('pipe', 'tensor'), may hold values from -5.5 to 0
- dt_bias: float32 [4, 128], P('pipe', 'tensor'), may hold values from -5 to -2
- d_skip: float32 [4, 128], P('pipe', 'tensor'), may hold values from 0.5 to 1.5
Outputs:
- grad_input: bfloat16 [4, 8, 192, 4096], P('pipe', 'dp', 'tensor')
- grad_out_weight: bfloat16 [4, 8192, 4096], P('pipe', 'tensor', 'dp')
- grad_conv_weight: float32 [4, 4, 12288], P('pipe', None, 'tensor')
- grad_conv_bias: float32 [4, 12288], P('pipe', 'tensor')
- grad_a_log: float32 [4, 128], P('pipe', 'tensor')
- grad_dt_bias: float32 [4, 128], P('pipe', 'tensor')
- grad_d_skip: float32 [4, 128], P('pipe', 'tensor')
All inputs are finite; a program needn't handle non-finite values.
Results may differ from a plain program's by a relative error of at most 0.025.
Values may be sent and summed in bfloat16 or wider, within the bound.
A program may use at most 192 MiB of HBM per device.

v0:
```python
import jax
import jax.numpy as jnp
from jax import lax
from jax.sharding import PartitionSpec as P

HEAD_DIM = 64
STATE = 256


HIGHEST_PRECISION = lax.Precision.HIGHEST


def shifted(value, axis, steps):
    count = lax.axis_size(axis)
    leading, last = (max(0, -steps), min(count, count - steps))
    return lax.ppermute(value, axis, [(source, source + steps) for source in range(leading, last)])


def mix_forward(inputs, raw_steps, taps, tap_bias, log_rates, step_bias, skip_gain, group_count):
    length = inputs.shape[0]
    width = taps.shape[0]
    padded = jnp.pad(inputs, ((width - 1, 0), (0, 0)))
    mixed = jnp.broadcast_to(tap_bias, inputs.shape)
    for offset in range(width):
        mixed = mixed + taps[offset] * padded[offset : offset + length]
    active = jax.nn.silu(mixed).reshape(length, group_count, -1)
    inner = active.shape[2] - 2 * STATE
    per_group = inner // HEAD_DIM
    values = active[:, :, :inner].reshape(length, group_count, per_group, HEAD_DIM)
    keys_b = active[:, :, inner : inner + STATE]
    query_c = active[:, :, inner + STATE :]
    deltas = jax.nn.softplus(raw_steps + step_bias).reshape(length, group_count, per_group)
    rates = -jnp.exp(log_rates).reshape(group_count, per_group)
    totals = jnp.cumsum(deltas * rates, axis=0)
    causal = (jnp.arange(length)[:, None] >= jnp.arange(length)[None, :])[:, :, None, None]
    spread = totals[:, None] - totals[None, :]
    decay = jnp.where(causal, jnp.exp(jnp.where(causal, spread, 0.0)), 0.0)
    intersection = jnp.einsum("tgn,sgn->tsg", query_c, keys_b, precision=HIGHEST_PRECISION)
    mixing = decay * intersection[:, :, :, None] * deltas[None]
    output = jnp.einsum("tsgh,sghp->tghp", mixing, values, precision=HIGHEST_PRECISION)
    output = output + skip_gain.reshape(group_count, per_group)[None, :, :, None] * values
    return output.reshape(length, -1)


def shards(
    cotangent,
    saved_u,
    dt_raw,
    in_weight,
    out_weight,
    conv_weight,
    conv_bias,
    a_log,
    dt_bias,
    d_skip,
):
    sections = lax.axis_size("pipe")
    section = lax.axis_index("pipe")
    micro = cotangent.shape[0]
    model_width = cotangent.shape[2]
    in_local = in_weight[0]
    out_local = out_weight[0]
    local_cols = in_local.shape[1]
    local_heads = a_log.shape[1]
    group_count = (local_cols - local_heads * HEAD_DIM) // (2 * STATE)
    is_last = section == sections - 1

    def work(grad_full, micro_no, active, carry):

        def busy(carry_in):
            inputs = lax.dynamic_index_in_dim(saved_u[0], micro_no, 0, keepdims=False).astype(
                jnp.float32
            )
            raw_now = lax.dynamic_index_in_dim(dt_raw[0], micro_no, 0, keepdims=False)

            def forward(values_in, taps, tap_bias, log_rates, step_bias, skip_gain):
                return mix_forward(
                    values_in, raw_now, taps, tap_bias, log_rates, step_bias, skip_gain, group_count
                )

            output, pull = jax.vjp(
                forward, inputs, conv_weight[0], conv_bias[0], a_log[0], dt_bias[0], d_skip[0]
            )
            output_low = output.astype(jnp.bfloat16)
            weight_acc = carry_in[0] + lax.dot_general(
                output_low, grad_full, (((0,), (0,)), ((), ())), preferred_element_type=jnp.float32
            )
            grad_mix = lax.dot_general(
                grad_full, out_local, (((1,), (1,)), ((), ())), preferred_element_type=jnp.float32
            ).astype(jnp.bfloat16)
            pulled = pull(lax.optimization_barrier(grad_mix).astype(jnp.float32))
            grad_inputs = pulled[0].astype(jnp.bfloat16)
            partial_rows = lax.dot_general(
                grad_inputs, in_local, (((1,), (1,)), ((), ())), preferred_element_type=jnp.float32
            )
            rest = tuple((old + new for old, new in zip(carry_in[1:], pulled[1:])))
            return (partial_rows, (weight_acc,) + rest)

        def quiet(carry_in):
            return (jnp.zeros((grad_full.shape[0], model_width), jnp.float32), carry_in)

        return lax.cond(active, busy, quiet, carry)

    carry = (
        jnp.zeros((out_local.shape[0], model_width), jnp.float32),
        jnp.zeros_like(conv_weight[0]),
        jnp.zeros_like(conv_bias[0]),
        jnp.zeros_like(a_log[0]),
        jnp.zeros_like(dt_bias[0]),
        jnp.zeros_like(d_skip[0]),
    )
    grad_buffer = jnp.zeros(cotangent.shape, jnp.bfloat16)
    incoming = jnp.zeros(cotangent.shape[1:], jnp.bfloat16)
    for tick in range(sections + micro - 1):
        micro_no = tick - (sections - 1 - section)
        active = (micro_no >= 0) & (micro_no < micro)
        picked = jnp.clip(micro_no, 0, micro - 1)
        grad_part = jnp.where(
            is_last, lax.dynamic_index_in_dim(cotangent, picked, 0, keepdims=False), incoming
        )
        grad_full = lax.all_gather(grad_part, "tensor", axis=0, tiled=True)
        partial_rows, carry = work(grad_full, picked, active, carry)
        reduced = lax.psum_scatter(partial_rows, "tensor", scatter_dimension=0, tiled=True)
        own_part = (grad_part.astype(jnp.float32) + reduced).astype(jnp.bfloat16)
        incoming = shifted(own_part, "pipe", -1)
        grad_buffer = jnp.where(
            active, lax.dynamic_update_index_in_dim(grad_buffer, own_part, picked, 0), grad_buffer
        )
    weight_part = lax.psum_scatter(
        carry[0].astype(jnp.bfloat16), "dp", scatter_dimension=1, tiled=True
    )
    summed = lax.psum((carry[1], carry[2], carry[3], carry[4], carry[5]), "dp")
    return (
        grad_buffer[None],
        weight_part[None],
        summed[0][None],
        summed[1][None],
        summed[2][None],
        summed[3][None],
        summed[4][None],
    )


def solution(mesh):
    return jax.shard_map(
        shards,
        mesh=mesh,
        in_specs=(
            P("dp", "tensor", None),
            P("pipe", "dp", None, "tensor"),
            P("pipe", "dp", None, "tensor"),
            P("pipe", None, "tensor"),
            P("pipe", "tensor", None),
            P("pipe", None, "tensor"),
            P("pipe", "tensor"),
            P("pipe", "tensor"),
            P("pipe", "tensor"),
            P("pipe", "tensor"),
        ),
        out_specs=(
            P("pipe", "dp", "tensor", None),
            P("pipe", "tensor", "dp"),
            P("pipe", None, "tensor"),
            P("pipe", "tensor"),
            P("pipe", "tensor"),
            P("pipe", "tensor"),
            P("pipe", "tensor"),
        ),
        check_vma=False,
    )
```

profile of v0, /device:TPU:0, one launch (start us, length us, event | category | flops | bytes accessed | tf_op | source)
XLA Modules:
  0.0 1258.2 jit_solution(15424770264920241005)
XLA Ops:
  8.9 54.1 %all-gather.15.cloned.1.call-done = bf16[1,192,4096]{2,1,0:T(8,128)(2,1)} async-done(((bf16[1,24,4096]{2,1,0:T(8,128)(2,1)}), bf16[1,192,4096]{2,1,0:T(8,128)(2,1)}) %all-gather.15.cloned.1.call-update) | async-done | bytes 1572880 | tf_op jit(solution)/shard_map/all_gather | solution.py:121
  63.0 19.6 %conditional.5 = (f32[192,4096]{1,0:T(8,128)}, f32[1024,4096]{1,0:T(8,128)}, f32[4,1536]{1,0:T(4,128)}, f32[1536]{0:T(1024)S(1)}, f32[16]{0:T(128)}, /*index=5*/f32[16]{0:T(128)}, f32[16]{0:T(128)}) conditional(s32[]{:T(128)} %convert_element_type.150, () %tuple.68, (f32[1,4,1536]{2,1,0:T(4,128)}, s32[]{:T(128)}, f32[1,2,192,16]{2,3,1,0:T(8,128)}, ...), branch_computations={%region_0.1_spmd, %region_1.20_spmd} | conditional | flops 7365856768 | bytes 103830472 | solution.py:102
  63.0 7.8 broadcast_in_dim.231
  82.7 119.7 %reduce-scatter.7.cloned.1.call-done = f32[24,4096]{1,0:T(8,128)} async-done(((f32[192,4096]{1,0:T(8,128)}), f32[24,4096]{1,0:T(8,128)}) %reduce-scatter.7.cloned.1.call-update) | async-done | bytes 393232 | tf_op jit(solution)/shard_map/reduce_scatter | solution.py:123
  206.2 2.0 collective-permute-done
  209.1 51.7 %all-gather.7.cloned.1.call-done = bf16[192,4096]{1,0:T(8,128)(2,1)} async-done(((bf16[24,4096]{1,0:T(8,128)(2,1)}), bf16[192,4096]{1,0:T(8,128)(2,1)}) %all-gather.7.cloned.1.call-update) | async-done | bytes 1572880 | tf_op jit(solution)/shard_map/all_gather | solution.py:121
  260.7 9.5 conditional.6
  270.3 174.9 %reduce-scatter.9.cloned.1.call-done = f32[24,4096]{1,0:T(8,128)} async-done(((f32[192,4096]{1,0:T(8,128)}), f32[24,4096]{1,0:T(8,128)}) %reduce-scatter.9.cloned.1.call-update) | async-done | bytes 393232 | tf_op jit(solution)/shard_map/reduce_scatter | solution.py:123
  451.1 51.6 %all-gather.9.cloned.1.call-done = bf16[192,4096]{1,0:T(8,128)(2,1)} async-done(((bf16[24,4096]{1,0:T(8,128)(2,1)}), bf16[192,4096]{1,0:T(8,128)(2,1)}) %all-gather.9.cloned.1.call-update) | async-done | bytes 1572880 | tf_op jit(solution)/shard_map/all_gather | solution.py:121
  502.8 9.2 conditional.7
  512.1 174.8 %reduce-scatter.11.cloned.1.call-done = f32[24,4096]{1,0:T(8,128)} async-done(((f32[192,4096]{1,0:T(8,128)}), f32[24,4096]{1,0:T(8,128)}) %reduce-scatter.11.cloned.1.call-update) | async-done | bytes 393232 | tf_op jit(solution)/shard_map/reduce_scatter | solution.py:123
  690.1 2.0 collective-permute-done.2
  692.9 51.7 %all-gather.11.cloned.1.call-done = bf16[192,4096]{1,0:T(8,128)(2,1)} async-done(((bf16[24,4096]{1,0:T(8,128)(2,1)}), bf16[192,4096]{1,0:T(8,128)(2,1)}) %all-gather.11.cloned.1.call-update) | async-done | bytes 1572880 | tf_op jit(solution)/shard_map/all_gather | solution.py:121
  744.6 106.1 %conditional.8 = (f32[192,4096]{1,0:T(8,128)}, f32[1024,4096]{1,0:T(8,128)}, f32[4,1536]{1,0:T(4,128)}, f32[1536]{0:T(1024)S(1)}, f32[16]{0:T(128)}, /*index=5*/f32[16]{0:T(128)}, f32[16]{0:T(128)}) conditional(s32[]{:T(128)} %convert_element_type.159, (f32[1024,4096]{1,0:T(8,128)}, f32[4,1536]{1,0:T(4,128)}, f32[1536]{0:T(1024)S(1)}, ...), branch_computations={%region_60.62_spmd, %region_61.0_spmd} | conditional | flops 7370058752 | bytes 111631048 | solution.py:102
  746.1 2.5 multiply_bitcast_fusion.6
  749.5 2.5 copy.183
  769.8 7.5 convolution_convert_fusion.3
  779.4 5.8 fusion.124
  785.8 4.2 reduce-window.64
  803.4 2.2 convolution_bitcast_fusion.10
  805.6 2.2 copy.184
  807.8 4.8 fusion.139
  812.6 2.5 copy.186
  815.1 2.7 multiply_reduce_fusion.18
  819.3 4.3 fusion.141
  823.6 14.2 %convolution_add_fusion.2 = f32[1024,4096]{1,0:T(8,128)} fusion(f32[1024,4096]{1,0:T(8,128)} %get-tuple-element.287, bf16[192,1024]{0,1:T(8,128)(2,1)S(1)} %bitcast.773, bf16[192,4096]{1,0:T(8,128)(2,1)S(1)} %copy-done.19), kind=kOutput, calls=%fused_computation.292 | convolution fusion | flops 1614807040 | bytes 35520512 | tf_op jit(solution)/shard_map/cond/branch_1_fun/dot_general | solution.py:85
  838.4 10.6 fusion.146
  850.8 77.6 %reduce-scatter.13.cloned.1.call-done = f32[24,4096]{1,0:T(8,128)} async-done(((f32[192,4096]{1,0:T(8,128)}), f32[24,4096]{1,0:T(8,128)}) %reduce-scatter.13.cloned.1.call-update) | async-done | bytes 393232 | tf_op jit(solution)/shard_map/reduce_scatter | solution.py:123
  931.6 2.0 collective-permute-done.3
  934.4 51.6 %all-gather.13.cloned.1.call-done = bf16[192,4096]{1,0:T(8,128)(2,1)} async-done(((bf16[24,4096]{1,0:T(8,128)(2,1)}), bf16[192,4096]{1,0:T(8,128)(2,1)}) %all-gather.13.cloned.1.call-update) | async-done | bytes 1572880 | tf_op jit(solution)/shard_map/all_gather | solution.py:121
  986.0 105.4 %conditional.9 = (f32[192,4096]{1,0:T(8,128)}, f32[1024,4096]{1,0:T(8,128)}, f32[4,1536]{1,0:T(4,128)}, f32[1536]{0:T(1024)S(1)}, f32[16]{0:T(128)}, /*index=5*/f32[16]{0:T(128)}, f32[16]{0:T(128)}) conditional(s32[]{:T(128)} %convert_element_type.162, (f32[1024,4096]{1,0:T(8,128)}, f32[4,1536]{1,0:T(4,128)}, f32[1536]{0:T(1024)S(1)}, ...), branch_computations={%region_80.82_spmd, %region_81.100_spmd} | conditional | flops 7370058752 | bytes 111631912 | solution.py:102
  987.4 2.5 multiply_bitcast_fusion.8
  990.9 2.5 copy.197
  1010.5 7.5 convolution_convert_fusion.4
  1020.1 5.7 fusion.164
  1026.5 4.0 reduce-window.76
  1044.1 2.2 convolution_bitcast_fusion.13
  1046.2 2.2 copy.198
  1048.4 4.7 fusion.179
  1053.1 2.4 copy.200
  1055.6 2.7 multiply_reduce_fusion.23
  1059.8 4.2 fusion.181
  1064.1 14.2 %convolution_add_fusion.3 = f32[1024,4096]{1,0:T(8,128)} fusion(f32[1024,4096]{1,0:T(8,128)} %get-tuple-element.312, bf16[192,1024]{0,1:T(8,128)(2,1)S(1)} %bitcast.774, bf16[192,4096]{1,0:T(8,128)(2,1)S(1)} %copy-done.16), kind=kOutput, calls=%fused_computation.390 | convolution fusion | flops 1614807040 | bytes 35520512 | tf_op jit(solution)/shard_map/cond/branch_1_fun/dot_general | solution.py:85
  1079.0 10.7 fusion.186
  1091.5 9.0 convert_element_type.164
  1101.6 18.3 %all-reduce.70 = (f32[1,4,1536]{2,1,0:T(4,128)}, f32[1,1536]{1,0:T(1,128)}, f32[1,16]{1,0:T(1,128)}, f32[1,16]{1,0:T(1,128)}, f32[1,16]{1,0:T(1,128)}) all-reduce(f32[1,4,1536]{2,1,0:T(4,128)} %bitcast.286, f32[1,1536]{1,0:T(1,128)S(1)} %broadcast_in_dim.315, ...), channel_id=1, replica_groups=mesh['pipe'=4,'tensor'=8,'dp'=4] {'dp'}, use_global_device_ids=true, to_apply=%region_101.103 | all-reduce | flops 7728 | bytes 61824 | tf_op jit(solution)/shard_map/psum | solution.py:132
  1119.9 49.2 %reduce-scatter.15.cloned.1.call-done = f32[24,4096]{1,0:T(8,128)} async-done(((f32[192,4096]{1,0:T(8,128)}), f32[24,4096]{1,0:T(8,128)}) %reduce-scatter.15.cloned.1.call-update) | async-done | bytes 393232 | tf_op jit(solution)/shard_map/reduce_scatter | solution.py:123
  1170.2 81.2 %reduce-scatter.17.cloned.1.call-done = bf16[1024,1024]{1,0:T(8,128)(2,1)} async-done(((bf16[1024,4096]{1,0:T(8,128)(2,1)}), bf16[1024,1024]{1,0:T(8,128)(2,1)}) %reduce-scatter.17.cloned.1.call-update) | async-done | bytes 2097168 | tf_op jit(solution)/shard_map/reduce_scatter | solution.py:129
  (240 shorter events, 110.1 us)
Async XLA Ops:
  7.2 55.9 %all-gather.15.cloned.1.call-start = ((), (), s32[]{:S(2)}) async-start(), calls=%async_computation.16 | async-start | bytes 1769472 | tf_op jit(solution)/shard_map/all_gather | solution.py:121
  8.9 193.5 %reduce-scatter.7.cloned.1.call-start = ((), (), s32[]{:S(2)}) async-start(), calls=%async_computation.6 | async-start | bytes 3538944 | tf_op jit(solution)/shard_map/reduce_scatter | solution.py:123
  82.6 120.6 %copy-start.8 = (bf16[2,24,4096]{2,1,0:T(8,128)(2,1)S(1)}, bf16[2,24,4096]{2,1,0:T(8,128)(2,1)}, u32[]{:S(2)}) copy-start(bf16[2,24,4096]{2,1,0:T(8,128)(2,1)} %param.21) | copy-start | bytes 1179652
  82.7 178.1 %copy-start = (bf16[1,2,192,1536]{3,2,1,0:T(8,128)(2,1)S(1)}, bf16[1,2,192,1536]{3,2,1,0:T(8,128)(2,1)}, u32[]{:S(2)}) copy-start(bf16[1,2,192,1536]{3,2,1,0:T(8,128)(2,1)} %param.22) | copy-start | bytes 3538948
  82.7 178.0 %copy-start.27 = (f32[1,4,1536]{2,1,0:T(4,128)S(1)}, f32[1,4,1536]{2,1,0:T(4,128)}, u32[]{:S(2)}) copy-start(f32[1,4,1536]{2,1,0:T(4,128)} %param.26) | copy-start | bytes 73732
  82.7 178.0 %copy-start.40 = (f32[1,1536]{1,0:T(1,128)S(1)}, f32[1,1536]{1,0:T(1,128)}, u32[]{:S(2)}) copy-start(f32[1,1536]{1,0:T(1,128)} %param.27) | copy-start | bytes 18436
  82.7 178.0 %all-gather.7.cloned.1.call-start = ((), (), s32[]{:S(2)}) async-start(), calls=%async_computation.7 | async-start | bytes 1769472 | tf_op jit(solution)/shard_map/all_gather | solution.py:121
  204.9 3.3 collective-permute-start
  209.0 236.2 %reduce-scatter.9.cloned.1.call-start = ((), (), s32[]{:S(2)}) async-start(), calls=%async_computation.8 | async-start | bytes 3538944 | tf_op jit(solution)/shard_map/reduce_scatter | solution.py:123
  270.2 175.0 %copy-start.13 = (bf16[24,4096]{1,0:T(8,128)(2,1)S(1)}, bf16[24,4096]{1,0:T(8,128)(2,1)}, u32[]{:S(2)}) copy-start(bf16[24,4096]{1,0:T(8,128)(2,1)} %bitcast_select_fusion.6) | copy-start | bytes 589828
  270.2 180.1 %copy-start.9 = (bf16[2,24,4096]{2,1,0:T(8,128)(2,1)S(1)}, bf16[2,24,4096]{2,1,0:T(8,128)(2,1)}, u32[]{:S(2)}) copy-start(bf16[2,24,4096]{2,1,0:T(8,128)(2,1)} %param.21) | copy-start | bytes 1179652
  270.2 232.5 %copy-start.28 = (f32[1,4,1536]{2,1,0:T(4,128)S(1)}, f32[1,4,1536]{2,1,0:T(4,128)}, u32[]{:S(2)}) copy-start(f32[1,4,1536]{2,1,0:T(4,128)} %param.26) | copy-start | bytes 73732
  270.2 232.5 %all-gather.9.cloned.1.call-start = ((), (), s32[]{:S(2)}) async-start(), calls=%async_computation.9 | async-start | bytes 1769472 | tf_op jit(solution)/shard_map/all_gather | solution.py:121
  447.0 3.3 collective-permute-start.1
  451.1 235.9 %reduce-scatter.11.cloned.1.call-start = ((), (), s32[]{:S(2)}) async-start(), calls=%async_computation.10 | async-start | bytes 3538944 | tf_op jit(solution)/shard_map/reduce_scatter | solution.py:123
  512.0 175.0 %copy-start.14 = (bf16[24,4096]{1,0:T(8,128)(2,1)S(1)}, bf16[24,4096]{1,0:T(8,128)(2,1)}, u32[]{:S(2)}) copy-start(bf16[24,4096]{1,0:T(8,128)(2,1)} %bitcast_select_fusion.4) | copy-start | bytes 589828
  512.1 180.1 %copy-start.10 = (bf16[2,24,4096]{2,1,0:T(8,128)(2,1)S(1)}, bf16[2,24,4096]{2,1,0:T(8,128)(2,1)}, u32[]{:S(2)}) copy-start(bf16[2,24,4096]{2,1,0:T(8,128)(2,1)} %param.21) | copy-start | bytes 1179652
  512.1 232.6 %copy-start.29 = (f32[1,4,1536]{2,1,0:T(4,128)S(1)}, f32[1,4,1536]{2,1,0:T(4,128)}, u32[]{:S(2)}) copy-start(f32[1,4,1536]{2,1,0:T(4,128)} %param.26) | copy-start | bytes 73732
  512.1 232.6 %all-gather.11.cloned.1.call-start = ((), (), s32[]{:S(2)}) async-start(), calls=%async_computation.11 | async-start | bytes 1769472 | tf_op jit(solution)/shard_map/all_gather | solution.py:121
  688.8 3.3 collective-permute-start.2
  692.9 235.6 %reduce-scatter.13.cloned.1.call-start = ((), (), s32[]{:S(2)}) async-start(), calls=%async_computation.12 | async-start | bytes 3538944 | tf_op jit(solution)/shard_map/reduce_scatter | solution.py:123
  779.4 5.8 copy-start.78
  815.0 4.2 copy-start.86
  819.3 4.3 copy-start.19
  823.6 14.3 %copy-start.56 = (f32[1536]{0:T(1024)S(1)}, f32[1536]{0:T(1024)}, u32[]{:S(2)}) copy-start(f32[1536]{0:T(1024)} %get-tuple-element.444) | copy-start | bytes 18436 | tf_op jit(solution)/shard_map/cond
  823.6 14.3 %copy-start.57 = (f32[1536]{0:T(1024)S(1)}, f32[1536]{0:T(1024)}, u32[]{:S(2)}) copy-start(f32[1536]{0:T(1024)} %get-tuple-element.445) | copy-start | bytes 18436 | tf_op jit(solution)/shard_map/cond
  823.6 14.2 %copy-start.58 = (f32[1536]{0:T(1024)S(1)}, f32[1536]{0:T(1024)}, u32[]{:S(2)}) copy-start(f32[1536]{0:T(1024)} %get-tuple-element.446) | copy-start | bytes 18436 | tf_op jit(solution)/shard_map/cond
  823.6 14.2 %copy-start.59 = (f32[1536]{0:T(1024)S(1)}, f32[1536]{0:T(1024)}, u32[]{:S(2)}) copy-start(f32[1536]{0:T(1024)} %get-tuple-element.447) | copy-start | bytes 18436 | tf_op jit(solution)/shard_map/cond
  838.4 10.6 copy-start.4
  850.7 77.7 %copy-start.15 = (bf16[24,4096]{1,0:T(8,128)(2,1)S(1)}, bf16[24,4096]{1,0:T(8,128)(2,1)}, u32[]{:S(2)}) copy-start(bf16[24,4096]{1,0:T(8,128)(2,1)} %bitcast_select_fusion.2) | copy-start | bytes 589828
  850.8 82.8 %copy-start.11 = (bf16[2,24,4096]{2,1,0:T(8,128)(2,1)S(1)}, bf16[2,24,4096]{2,1,0:T(8,128)(2,1)}, u32[]{:S(2)}) copy-start(bf16[2,24,4096]{2,1,0:T(8,128)(2,1)} %param.21) | copy-start | bytes 1179652
  850.8 135.2 %copy-start.30 = (f32[1,4,1536]{2,1,0:T(4,128)S(1)}, f32[1,4,1536]{2,1,0:T(4,128)}, u32[]{:S(2)}) copy-start(f32[1,4,1536]{2,1,0:T(4,128)} %param.26) | copy-start | bytes 73732
  850.8 135.2 %all-gather.13.cloned.1.call-start = ((), (), s32[]{:S(2)}) async-start(), calls=%async_computation.13 | async-start | bytes 1769472 | tf_op jit(solution)/shard_map/all_gather | solution.py:121
  930.3 3.3 collective-permute-start.3
  934.3 234.8 %reduce-scatter.15.cloned.1.call-start = ((), (), s32[]{:S(2)}) async-start(), calls=%async_computation.14 | async-start | bytes 3538944 | tf_op jit(solution)/shard_map/reduce_scatter | solution.py:123
  990.9 5.2 copy-start.92
  990.9 5.7 copy-start.73
  1020.1 5.8 copy-start.80
  1042.1 6.3 copy-start.101
  1059.8 4.3 copy-start.16
  1064.1 14.3 %copy-start.60 = (f32[1536]{0:T(1024)S(1)}, f32[1536]{0:T(1024)}, u32[]{:S(2)}) copy-start(f32[1536]{0:T(1024)} %get-tuple-element.457) | copy-start | bytes 18436 | tf_op jit(solution)/shard_map/cond
  1064.1 14.3 %copy-start.61 = (f32[1536]{0:T(1024)S(1)}, f32[1536]{0:T(1024)}, u32[]{:S(2)}) copy-start(f32[1536]{0:T(1024)} %get-tuple-element.458) | copy-start | bytes 18436 | tf_op jit(solution)/shard_map/cond
  1064.1 14.3 %copy-start.62 = (f32[1536]{0:T(1024)S(1)}, f32[1536]{0:T(1024)}, u32[]{:S(2)}) copy-start(f32[1536]{0:T(1024)} %get-tuple-element.459) | copy-start | bytes 18436 | tf_op jit(solution)/shard_map/cond
  1064.1 14.3 %copy-start.63 = (f32[1536]{0:T(1024)S(1)}, f32[1536]{0:T(1024)}, u32[]{:S(2)}) copy-start(f32[1536]{0:T(1024)} %get-tuple-element.460) | copy-start | bytes 18436 | tf_op jit(solution)/shard_map/cond
  1079.0 10.7 copy-start.5
  1091.5 160.0 %reduce-scatter.17.cloned.1.call-start = ((), (), s32[]{:S(2)}) async-start(), calls=%async_computation.15 | async-start | bytes 10485760 | tf_op jit(solution)/shard_map/reduce_scatter | solution.py:129
  1100.5 68.6 %copy-start.12 = (bf16[24,4096]{1,0:T(8,128)(2,1)S(1)}, bf16[24,4096]{1,0:T(8,128)(2,1)}, u32[]{:S(2)}) copy-start(bf16[24,4096]{1,0:T(8,128)(2,1)} %bitcast_select_fusion) | copy-start | bytes 589828
  1170.2 81.2 %copy-start.33 = (bf16[1,2,24,4096]{3,2,1,0:T(8,128)(2,1)}, bf16[1,2,24,4096]{3,2,1,0:T(8,128)(2,1)S(1)}, u32[]{:S(2)}) copy-start(bf16[1,2,24,4096]{3,2,1,0:T(8,128)(2,1)S(1)} %fusion.203) | copy-start | bytes 1179652
  (13 other events, 47.4 us)
Sparse Core Ops, SparseCore 0:
  10.9 52.1 all-gather.14
  82.8 119.5 reduce-scatter.6
  209.1 51.5 all-gather.6
  270.3 174.7 reduce-scatter.8
  451.2 51.5 all-gather.8
  512.2 174.7 reduce-scatter.10
  693.0 51.5 all-gather.10
  850.9 77.5 reduce-scatter.12
  934.4 51.5 all-gather.12
  1091.6 77.4 reduce-scatter.14
  1172.2 79.2 reduce-scatter.16
where the time goes:
time: 1270 us; the launch traced here: 1260 us
  waiting for transfers between devices  946 us (74%)
  matrix products  104 us (8%)
  local copies, waits for them, and re-layouts  75.1 us (6%)
  other arithmetic  71 us (6%)
  loops' own time  23.1 us (2%)
  blocking collectives  18.3 us (1%)
  between operations  14.4 us (1%)
    reduce_scatter x5, waiting for transfers between devices, shards(): lax.psum_scatter(partial_rows, 'tensor', scatter_dimension=0, tiled=True)  596 us
    all_gather x5, waiting for transfers between devices, shards(): grad_full = lax.all_gather(grad_part, 'tensor', axis=0, tiled=True)  261 us
    reduce_scatter x1, waiting for transfers between devices, shards(): lax.psum_scatter(carry[0].astype(jnp.bfloat16), 'dp', scatter_dimension=1...  81.2 us
    another operation x38, local copies, waits for them, and re-layouts  37.2 us
    dot_general x6, matrix products, mix_forward(): jnp.einsum('tsgh,sghp->tghp', mixing, values, precision=HIGHEST_PRECISION)  29.5 us
    dot_general x2, matrix products, busy(): lax.dot_general(output_low, grad_full, (((0,), (0,)), ((), ())), preferre...  28.5 us
  transfers between devices with their start and end apart: 15, of which 15 were waited for; matrix products, arithmetic and copies ran while one was open for 1% of the time, Pallas kernels for 0%

commit v1 on v0

v1 whole, which is shorter than its diff:
```python
import jax
import jax.numpy as jnp
from jax import lax
from jax.experimental import pallas as pl
from jax.experimental.pallas import tpu as pltpu
from jax.sharding import PartitionSpec as P

F32 = jnp.float32
BF16 = jnp.bfloat16
MESH = pl.DeviceIdType.MESH
NT = (((1,), (1,)), ((), ()))
NN = (((1,), (0,)), ((), ()))
TN = (((0,), (0,)), ((), ()))
HIGH = lax.Precision.HIGHEST

L = 192
D = 4096
X = 1024
C = 1536
HEADS = 16
PAIRS = 8
N = 256
T = 8
W = D // T
R = L // T
DP = 4
S = 2
TOP = 8


def dot(a, b, dims, precision=None):
    return lax.dot_general(a, b, dims, preferred_element_type=F32, precision=precision)


def iota(shape, axis):
    return lax.broadcasted_iota(jnp.int32, shape, axis)


def lanes(j, width=128):
    return pl.ds(pl.multiple_of(j * width, width), width)


def loop(count, body):
    def step(i, carry):
        body(i)
        return carry

    lax.fori_loop(0, count, step, 0)


def kernel(
    cot_ref, u_hbm, win_hbm, wout_hbm, dtr_ref, cw_ref, cb_ref, al_ref, db_ref, sk_ref,
    gi_out, gow_out, pg_out,
    win, wout, u_ref, upad, sp, abf, xst, mt, est, y0, yb, sT, scol, dtc, skl,
    cbuf, crecv, gbuf, gcols, dyacc, dybf, dx0, dcb, dcpad, dubf, own,
    sbuf, rbuf, opart, obuf, girecv, gi_v, pg, pgr, pgsum,
    loc, cs_s, cs_r, g_s, g_r, rs_s, rs_r, ox_s, ox_r, yb_s, yb_r, gx_s, gx_r, pg_s, pg_r,
):
    p = lax.axis_index("pipe")
    t = lax.axis_index("tensor")
    d = lax.axis_index("dp")
    first = p == 3
    last = p == 0

    def peer(i):
        return (p, lax.rem(t + i, T), d)

    def replica(i):
        return (p, t, lax.rem(d + i, DP))

    def local(src, dst, i):
        return pltpu.make_async_copy(src, dst, loc.at[i])

    def remote(src, dst, ssem, rsem, to):
        return pltpu.make_async_remote_copy(
            src_ref=src, dst_ref=dst, send_sem=ssem, recv_sem=rsem, device_id=to, device_id_type=MESH
        )

    local(u_hbm, u_ref, 0).start()
    local(wout_hbm, wout, 1).start()
    local(win_hbm, win, 2).start()

    barrier = pltpu.get_barrier_semaphore()
    for i in range(1, T):
        pl.semaphore_signal(barrier, inc=1, device_id=peer(i), device_id_type=MESH)
    for i in range(1, DP):
        pl.semaphore_signal(barrier, inc=1, device_id=replica(i), device_id_type=MESH)

    @pl.when(p > 0)
    def _():
        for i in range(T):
            pl.semaphore_signal(barrier, inc=1, device_id=(p - 1, i, d), device_id_type=MESH)

    @pl.when(p < 3)
    def _():
        for i in range(T):
            pl.semaphore_signal(barrier, inc=1, device_id=(p + 1, i, d), device_id_type=MESH)

    middle = jnp.logical_and(p > 0, p < 3)

    @pl.when(middle)
    def _():
        pl.semaphore_wait(barrier, T - 1 + DP - 1 + 2 * T)

    @pl.when(jnp.logical_not(middle))
    def _():
        pl.semaphore_wait(barrier, T - 1 + DP - 1 + T)

    def cot_copy(s, i):
        return remote(cbuf.at[s], crecv.at[s, t], cs_s.at[s, i - 1], cs_r.at[s, i - 1], peer(i))

    def cot_arrival(s, i):
        src = lax.rem(t + T - i, T)
        return remote(cbuf.at[s], crecv.at[s, src], cs_s.at[s, i - 1], cs_r.at[s, i - 1], peer(i))

    @pl.when(first)
    def _():
        for s in range(S):
            cbuf[s] = cot_ref[s]
            for i in range(1, T):
                cot_copy(s, i).start()
            crecv[s, t] = cot_ref[s]

    rr = iota((L, L), 0)
    tt = iota((L, L), 1)
    lower = (rr >= tt).astype(F32)
    upper = (rr <= tt).astype(F32)
    rate = -jnp.exp(al_ref[...])
    spread = (iota((HEADS, X), 0) == iota((HEADS, X), 1) // 64).astype(F32)
    skl[...] = dot(sk_ref[...], spread, NN, HIGH)

    def forward(s):
        upad[s, 0:TOP, :] = jnp.zeros((TOP, C), F32)

        def conv(j):
            at = lanes(j)
            upad[s, TOP : TOP + L, at] = u_ref[s, :, at].astype(F32)
            c = jnp.broadcast_to(cb_ref[:, at], (L, 128))
            for k in range(4):
                c = c + cw_ref[k : k + 1, at] * upad[s, TOP - 3 + k : TOP - 3 + k + L, at]
            sig = 1.0 / (1.0 + jnp.exp(-c))
            sp[s, :, at] = sig * (1.0 + c * (1.0 - sig))
            abf[s, :, at] = (c * sig).astype(BF16)

        loop(C // 128, conv)
        z = dtr_ref[s] + db_ref[...]
        dt = jnp.maximum(z, 0.0) + jnp.log1p(jnp.exp(-jnp.abs(z)))
        dtc[s] = dt
        dta = dt * rate
        scol[...] = dot(lower, dta, NN, HIGH)
        sT[...] = dot(dta, upper, TN, HIGH)
        dcb[...] = dot(abf[s, :, X : X + N], abf[s, :, X + N : X + 2 * N], NT)

        def pair(j):
            at = lanes(j)
            x2 = abf[s, :, at].astype(F32)
            even = iota((L, 128), 1) < 64
            xst[s, j, 0:L, :] = jnp.where(even, x2, 0.0).astype(BF16)
            xst[s, j, L : 2 * L, :] = jnp.where(even, 0.0, x2).astype(BF16)
            causal = iota((L, L), 1) >= iota((L, L), 0)
            head = iota((L, HEADS), 1)
            for e in range(2):
                h = 2 * j + e
                s_r = jnp.sum(jnp.where(head == h, scol[...], 0.0), axis=1, keepdims=True)
                dt_r = jnp.sum(jnp.where(head == h, dtc[s], 0.0), axis=1, keepdims=True)
                decay = jnp.exp(jnp.minimum(sT[pl.ds(h, 1), :] - s_r, 0.0)) * dt_r
                decay = jnp.where(causal, decay, 0.0)
                est[s, j, e * L : (e + 1) * L, :] = decay.astype(BF16)
                mt[s, j, e * L : (e + 1) * L, :] = (decay * dcb[...]).astype(BF16)
            y2 = dot(mt[s, j], xst[s, j], TN)
            y0[s, :, at] = y2
            yb[d, s, :, at] = (y2 + skl[:, at] * x2).astype(BF16)

        loop(PAIRS, pair)

    def yb_copy(s, i):
        return remote(yb.at[d, s], yb.at[d, s], yb_s.at[s, i - 1], yb_r.at[s, i - 1], replica(i))

    def yb_arrival(s, i):
        src = lax.rem(d + DP - i, DP)
        return remote(yb.at[src, s], yb.at[src, s], yb_s.at[s, i - 1], yb_r.at[s, i - 1], replica(i))

    local(u_hbm, u_ref, 0).wait()
    for s in range(S):
        forward(s)
        for i in range(1, DP):
            yb_copy(s, i).start()

    local(wout_hbm, wout, 1).wait()
    local(win_hbm, win, 2).wait()

    def g_arrival(s, k):
        return remote(gbuf.at[s, k], gbuf.at[s, k], g_s.at[s, 0], g_r.at[s, k], peer(1))

    def gx_copy(s, i):
        to = lax.rem(d + i, DP)
        return remote(
            gbuf.at[s, pl.ds(2 * to, 2)], gcols.at[d, s], gx_s.at[s, i - 1], gx_r.at[s, i - 1], replica(i)
        )

    def gx_arrival(s, i):
        src = lax.rem(d + DP - i, DP)
        return remote(
            gbuf.at[s, pl.ds(0, 2)], gcols.at[src, s], gx_s.at[s, i - 1], gx_r.at[s, i - 1], replica(i)
        )

    def grad_mix(s):
        @pl.when(first)
        def _():
            for i in range(1, T):
                cot_arrival(s, i).wait_recv()

            def block(k):
                rows = crecv[s, :, :, lanes(k, W)].astype(F32)
                gbuf[s, k] = rows.reshape(L, W).astype(BF16)

            loop(T, block)

        dyacc[...] = jnp.zeros_like(dyacc)

        def block(i):
            k = lax.rem(t + i, T)

            @pl.when(p < 3)
            def _():
                g_arrival(s, k).wait_recv()

            dyacc[...] += dot(gbuf[s, k], wout[:, lanes(k, W)], NT)

        loop(T, block)
        dybf[...] = dyacc[...].astype(BF16)
        for i in range(1, DP):
            gx_copy(s, i).start()
        gcols[d, s] = gbuf[s, pl.ds(2 * d, 2)]

    def pull(s):
        dcb[...] = jnp.zeros_like(dcb)

        def pair(j):
            at = lanes(j)
            dy2 = dybf[:, at]
            dm = dot(xst[s, j], dy2, NT)
            dcb[...] += dm[:L] * est[s, j, 0:L, :].astype(F32) + dm[L:] * est[s, j, L : 2 * L, :].astype(F32)
            dx = dot(mt[s, j], dy2, NN)
            dx = jnp.where(iota((L, 128), 1) < 64, dx[:L], dx[L:])
            dx0[:, at] = dx
            dcpad[0:L, at] = (dx + skl[:, at] * dy2.astype(F32)) * sp[s, :, at]

        loop(PAIRS, pair)
        low = dcb[...].astype(BF16)
        dcpad[0:L, X : X + N] = dot(low, abf[s, :, X + N : X + 2 * N], NN) * sp[s, :, X : X + N]
        dcpad[0:L, X + N : X + 2 * N] = (
            dot(low, abf[s, :, X : X + N], TN) * sp[s, :, X + N : X + 2 * N]
        )

        def conv(j):
            at = lanes(j)
            du = cw_ref[3:4, at] * dcpad[0:L, at]
            for k in range(3):
                du = du + cw_ref[k : k + 1, at] * dcpad[3 - k : 3 - k + L, at]
            dubf[:, at] = du.astype(BF16)

        loop(C // 128, conv)

    def rs_copy(s, j):
        return remote(sbuf.at[j], rbuf.at[s, j], rs_s.at[s, j], rs_r.at[s, j], peer(1 + j))

    def scatter(s):
        def block(j):
            k = lax.rem(t + 1 + j, T)
            part = dot(dubf[...], win[lanes(k, W), :], NT)
            sbuf[j] = part.astype(BF16)
            rs_copy(s, j).start()

        loop(T - 1, block)
        own[...] = dot(dubf[...], win[lanes(t, W), :], NT)

    def g_copy(s, i):
        return remote(opart.at[s], gbuf.at[s, t], g_s.at[s, i], g_r.at[s, t], (p - 1, i, d))

    def ox_copy(s, i):
        return remote(
            obuf.at[s, lax.rem(t + i, T)], girecv.at[s, t], ox_s.at[s, i - 1], ox_r.at[s, i - 1], peer(i)
        )

    def ox_arrival(s, i):
        src = lax.rem(t + T - i, T)
        return remote(obuf.at[s, src], girecv.at[s, src], ox_s.at[s, i - 1], ox_r.at[s, i - 1], peer(i))

    def reduce(s):
        loop(T - 1, lambda j: rs_copy(s, j).wait_recv())

        def block(j):
            at = lanes(j)
            total = own[:, at] + gbuf[s, t, :, at].astype(F32)
            for i in range(T - 1):
                total = total + rbuf[s, i, :, at].astype(F32)
            opart[s, :, at] = total.astype(BF16)
            obuf[s, :, :, at] = total.reshape(T, R, 128).astype(BF16)

        loop(W // 128, block)

        @pl.when(p > 0)
        def _():
            for i in range(T):
                g_copy(s, i).start()

        for i in range(1, T):
            ox_copy(s, i).start()
        girecv[s, t] = obuf[s, t]
        loop(T - 1, lambda j: rs_copy(s, j).wait_send())

    def parameters(s):
        def two(value):
            high = value.astype(BF16)
            rest = (value - high.astype(F32)).astype(BF16)
            return jnp.concatenate([high, rest], axis=1)

        def pair(j, carry):
            d_s, d_t, d_k = carry
            at = lanes(j)
            dy2 = dybf[:, at].astype(F32)
            x2 = abf[s, :, at].astype(F32)
            inner = x2 * dx0[:, at]
            outer = dy2 * y0[s, :, at] - inner
            lane = iota((2 * 128, HEADS), 0)
            lane = jnp.where(lane >= 128, lane - 128, lane)
            head = 2 * j + jnp.where(lane >= 64, 1, 0)
            pick = (head == iota((2 * 128, HEADS), 1)).astype(BF16)
            skip = jnp.broadcast_to(jnp.sum(dy2 * x2, axis=0, keepdims=True), (8, 128))
            return (
                d_s + dot(two(outer), pick, NN),
                d_t + dot(two(inner), pick, NN),
                d_k + dot(two(skip), pick, NN),
            )

        zero = jnp.zeros((L, HEADS), F32)
        d_s, d_t, d_k = lax.fori_loop(0, PAIRS, pair, (zero, zero, jnp.zeros((8, HEADS), F32)))
        later = dot((iota((L, L), 0) <= iota((L, L), 1)).astype(F32), d_s, NN, HIGH)
        dt = dtc[s]
        z = dtr_ref[s] + db_ref[...]
        g_al = jnp.sum(later * dt, axis=0, keepdims=True) * rate
        g_db = jnp.sum((d_t / dt + later * rate) / (1.0 + jnp.exp(-z)), axis=0, keepdims=True)
        small = (g_al, g_db, d_k[0:1])

        def conv(j):
            at = lanes(j)
            dc = dcpad[0:L, at]
            rows = []
            for k in range(4):
                rows.append(jnp.sum(dc * upad[s, TOP - 3 + k : TOP - 3 + k + L, at], axis=0, keepdims=True))
            rows.append(jnp.sum(dc, axis=0, keepdims=True))
            rows.append(jnp.zeros((3, 128), F32))
            value = jnp.concatenate(rows, axis=0)
            pg[:, at] = value if s == 0 else pg[:, at] + value

        loop(C // 128, conv)
        for i in range(3):
            if s == 0:
                pg[5 + i : 6 + i, 0:HEADS] = small[i]
            else:
                pg[5 + i : 6 + i, 0:HEADS] += small[i]

    def pg_copy(i):
        return remote(pg, pgr.at[d], pg_s.at[i - 1], pg_r.at[i - 1], replica(i))

    def pg_arrival(i):
        src = lax.rem(d + DP - i, DP)
        return remote(pg, pgr.at[src], pg_s.at[i - 1], pg_r.at[i - 1], replica(i))

    def projection():
        for s in range(S):
            for i in range(1, DP):
                yb_arrival(s, i).wait_recv()
                gx_arrival(s, i).wait_recv()

        for q in range(2):

            def block(j):
                rows = yb[:, :, :, lanes(j, 256)].reshape(DP * S * L, 256)
                cols = gcols[:, :, q].reshape(DP * S * L, W)
                win[lanes(j, 256), q * W : (q + 1) * W] = dot(rows, cols, TN).astype(BF16)

            loop(X // 256, block)
        local(win.at[pl.ds(0, X), pl.ds(0, X)], gow_out, 3).start()

    dcpad[L : L + TOP, :] = jnp.zeros((TOP, C), F32)
    grad_mix(0)
    pull(0)
    scatter(0)
    parameters(0)

    @pl.when(p < 3)
    def _():
        reduce(0)

    grad_mix(1)
    pull(1)

    @pl.when(first)
    def _():
        reduce(0)

    scatter(1)
    parameters(1)
    pgr[d] = pg[...]
    for i in range(1, DP):
        pg_copy(i).start()

    @pl.when(last)
    def _():
        projection()

    reduce(1)

    @pl.when(p > 0)
    def _():
        projection()

    for i in range(1, DP):
        pg_arrival(i).wait_recv()
    total = pgr[0]
    for i in range(1, DP):
        total = total + pgr[i]
    pgsum[...] = total
    local(pgsum, pg_out, 4).start()
    for s in range(S):
        for i in range(1, T):
            ox_arrival(s, i).wait_recv()
        for k in range(T):
            gi_v[s, :, k * W : (k + 1) * W] = girecv[s, k]
    local(gi_v, gi_out, 5).start()

    @pl.when(first)
    def _():
        for s in range(S):
            for i in range(1, T):
                cot_copy(s, i).wait_send()

    @pl.when(p > 0)
    def _():
        for s in range(S):
            for i in range(T):
                g_copy(s, i).wait_send()

    for s in range(S):
        for i in range(1, T):
            ox_copy(s, i).wait_send()
        for i in range(1, DP):
            yb_copy(s, i).wait_send()
            gx_copy(s, i).wait_send()
    for i in range(1, DP):
        pg_copy(i).wait_send()
    local(win.at[pl.ds(0, X), pl.ds(0, X)], gow_out, 3).wait()
    local(pgsum, pg_out, 4).wait()
    local(gi_v, gi_out, 5).wait()


def shards(cot, saved_u, dt_raw, in_weight, out_weight, conv_weight, conv_bias, a_log, dt_bias, d_skip):
    any_spec = pl.BlockSpec(memory_space=pl.ANY)
    vmem_spec = pl.BlockSpec(memory_space=pltpu.VMEM)
    sem = pltpu.SemaphoreType.DMA
    scratch = [
        pltpu.VMEM((D, C), BF16),
        pltpu.VMEM((X, D), BF16),
        pltpu.VMEM((S, L, C), BF16),
        pltpu.VMEM((S, L + 2 * TOP, C), F32),
        pltpu.VMEM((S, L, C), F32),
        pltpu.VMEM((S, L, C), BF16),
        pltpu.VMEM((S, PAIRS, 2 * L, 128), BF16),
        pltpu.VMEM((S, PAIRS, 2 * L, L), BF16),
        pltpu.VMEM((S, PAIRS, 2 * L, L), BF16),
        pltpu.VMEM((S, L, X), F32),
        pltpu.VMEM((DP, S, L, X), BF16),
        pltpu.VMEM((HEADS, L), F32),
        pltpu.VMEM((L, HEADS), F32),
        pltpu.VMEM((S, L, HEADS), F32),
        pltpu.VMEM((1, X), F32),
        pltpu.VMEM((S, R, D), BF16),
        pltpu.VMEM((S, T, R, D), BF16),
        pltpu.VMEM((S, T, L, W), BF16),
        pltpu.VMEM((DP, S, 2, L, W), BF16),
        pltpu.VMEM((L, X), F32),
        pltpu.VMEM((L, X), BF16),
        pltpu.VMEM((L, X), F32),
        pltpu.VMEM((L, L), F32),
        pltpu.VMEM((L + TOP, C), F32),
        pltpu.VMEM((L, C), BF16),
        pltpu.VMEM((L, W), F32),
        pltpu.VMEM((T - 1, L, W), BF16),
        pltpu.VMEM((S, T - 1, L, W), BF16),
        pltpu.VMEM((S, L, W), BF16),
        pltpu.VMEM((S, T, R, W), BF16),
        pltpu.VMEM((S, T, R, W), BF16),
        pltpu.VMEM((S, R, D), BF16),
        pltpu.VMEM((8, C), F32),
        pltpu.VMEM((DP, 8, C), F32),
        pltpu.VMEM((8, C), F32),
        sem((6,)),
        sem((S, T - 1)), sem((S, T - 1)),
        sem((S, T)), sem((S, T)),
        sem((S, T - 1)), sem((S, T - 1)),
        sem((S, T - 1)), sem((S, T - 1)),
        sem((S, DP - 1)), sem((S, DP - 1)),
        sem((S, DP - 1)), sem((S, DP - 1)),
        sem((DP - 1,)), sem((DP - 1,)),
    ]
    gi, gow, pg = pl.pallas_call(
        kernel,
        out_shape=(
            jax.ShapeDtypeStruct((S, R, D), BF16),
            jax.ShapeDtypeStruct((X, X), BF16),
            jax.ShapeDtypeStruct((8, C), F32),
        ),
        in_specs=[vmem_spec, any_spec, any_spec, any_spec] + [vmem_spec] * 6,
        out_specs=(any_spec, any_spec, any_spec),
        scratch_shapes=scratch,
        compiler_params=pltpu.CompilerParams(
            collective_id=0, has_side_effects=True, vmem_limit_bytes=64 * 2**20 - 2**16
        ),
        name="mixer_backward",
    )(cot, saved_u[0], in_weight[0], out_weight[0], dt_raw[0], conv_weight[0], conv_bias, a_log, dt_bias, d_skip)
    return (
        gi[None],
        gow[None],
        pg[None, 0:4],
        pg[4:5],
        pg[5:6, :HEADS],
        pg[6:7, :HEADS],
        pg[7:8, :HEADS],
    )


def solution(mesh):
    return jax.shard_map(
        shards,
        mesh=mesh,
        in_specs=(
            P("dp", "tensor", None),
            P("pipe", "dp", None, "tensor"),
            P("pipe", "dp", None, "tensor"),
            P("pipe", None, "tensor"),
            P("pipe", "tensor", None),
            P("pipe", None, "tensor"),
            P("pipe", "tensor"),
            P("pipe", "tensor"),
            P("pipe", "tensor"),
            P("pipe", "tensor"),
        ),
        out_specs=(
            P("pipe", "dp", "tensor", None),
            P("pipe", "tensor", "dp"),
            P("pipe", None, "tensor"),
            P("pipe", "tensor"),
            P("pipe", "tensor"),
            P("pipe", "tensor"),
            P("pipe", "tensor"),
        ),
        check_vma=False,
    )
```

time: 1270 us -> 224 us (0.18)
  waiting for transfers between devices: 946 us -> 0 us
  Pallas kernels: 0 us -> 210 us
  matrix products: 104 us -> 0 us
  other arithmetic: 71 us -> 0 us
  local copies, waits for them, and re-layouts: 75.1 us -> 10.5 us
  loops' own time: 23.1 us -> 0 us
  blocking collectives: 18.3 us -> 0 us
  between operations: 14.4 us -> 0.64 us
    reduce_scatter x6 -> x0, waiting for transfers between devices: 677 us -> none  [the longest x5 596 us: shards(): lax.psum_scatter(partial_rows, 'tensor', scatter_dimension=0, tiled=True)]
    all_gather x5 -> x0, waiting for transfers between devices: 261 us -> none  [shards(): grad_full = lax.all_gather(grad_part, 'tensor', axis=0, tiled=True)]
    pallas_call x0 -> x1, Pallas kernels: none -> 210 us  [shards(): pl.pallas_call(kernel, out_shape=(jax.ShapeDtypeStruct((S, R, D), BF16),...]
    dot_general x18 -> x0, matrix products: 104 us -> none  [the longest x6 29.5 us: mix_forward(): jnp.einsum('tsgh,sghp->tghp', mixing, values, precision=HIGHEST_PRECISION)]
    another operation x38 -> x0, local copies, waits for them, and re-layouts: 37.2 us -> none
    another operation x5 -> x0, loops' own time: 23.1 us -> none  [work(): return lax.cond(active, busy, quiet, carry)]
    another operation x16 -> x0, other arithmetic: 21 us -> none
    psum x1 -> x0, blocking collectives: 18.3 us -> none  [shards(): summed = lax.psum((carry[1], carry[2], carry[3], carry[4], carry[5]), 'dp')]
  transfers between devices with their start and end apart: 15 -> 0, of which waited for: 15 -> 0; matrix products, arithmetic and copies ran while one was open for 1% -> 0% of each run, Pallas kernels for 0% -> 0%
where the time goes in v1:
time: 224 us; the launch traced here: 221 us
  Pallas kernels  210 us (94%)
  local copies, waits for them, and re-layouts  10.5 us (5%)
    pallas_call x1, Pallas kernels, shards(): pl.pallas_call(kernel, out_shape=(jax.ShapeDtypeStruct((S, R, D), BF16),...  210 us
    unnamed x3, local copies, waits for them, and re-layouts  6.4 us

profile of v1, /device:TPU:0, one launch (start us, length us, event | category | flops | bytes accessed | tf_op | source)
XLA Modules:
  0.0 220.9 jit_solution(8965183912095838145)
XLA Ops:
  0.6 1.6 copy.17
  2.2 209.7 %mixer_backward.1 = (bf16[2,24,4096]{2,1,0:T(8,128)(2,1)}, bf16[1024,1024]{1,0:T(8,128)(2,1)}, f32[8,1536]{1,0:T(8,128)}) custom-call(bf16[2,24,4096]{2,1,0:T(8,128)(2,1)} %cot_ref.1, bf16[2,192,1536]{2,1,0:T(8,128)(2,1)} %bitcast.12, bf16[4096,1536]{1,0:T(8,128)(2,1)} %bitcast.9, bf16[1024,4096]{1,0:T(8,128)(2,1)} %bitcast.10, f32[2,192,16]{2,1,0:T(8,128)} %bitcast.13, ...), custom_call_target="tpu_custom_call" | custom-call | tf_op jit(solution)/shard_map/mixer_backward/pallas_call | solution.py:508
  211.9 1.3 fusion
  213.2 1.4 slice_bitcast_fusion
  214.6 1.4 slice.16
  216.0 1.8 copy.20
  217.8 3.1 %copy.21 = bf16[1,1024,1024]{2,1,0:T(8,128)(2,1)} copy(bf16[1,1024,1024]{2,1,0:T(8,128)(2,1)} %bitcast.11) | data formatting | bytes 4194304

commit v2 on v1

--- a/solution.py
+++ b/solution.py
@@ -21,7 +21,10 @@
 PAIRS = 8
 N = 256
 T = 8
-W = D // T
+Z = 4
+Q = 4
+B = Z * Q
+W = D // B
 R = L // T
 DP = 4
 S = 2
@@ -51,10 +54,11 @@
 def kernel(
     cot_ref, u_hbm, win_hbm, wout_hbm, dtr_ref, cw_ref, cb_ref, al_ref, db_ref, sk_ref,
     gi_out, gow_out, pg_out,
-    win, wout, u_ref, upad, sp, abf, xst, mt, est, y0, yb, sT, scol, dtc, skl,
+    win, wout, u_ref, upad, sp, abf, xst, mt, est, y0, yb, sT, scol, dtc, sgc, skl,
     cbuf, crecv, gbuf, gcols, dyacc, dybf, dx0, dcb, dcpad, dubf, own,
-    sbuf, rbuf, opart, obuf, girecv, gi_v, pg, pgr, pgsum,
-    loc, cs_s, cs_r, g_s, g_r, rs_s, rs_r, ox_s, ox_r, yb_s, yb_r, gx_s, gx_r, pg_s, pg_r,
+    sbuf, rbuf, psum, pbuf, orow, obuf, grecv, gi_v, pg, pgr, pgsum,
+    loc, cs_s, cs_r, a_s, a_r, b_s, b_r, c_s, c_r, f_s, f_r, o_s, o_r,
+    yb_s, yb_r, gx_s, gx_r, pg_s, pg_r,
 ):
     p = lax.axis_index("pipe")
     t = lax.axis_index("tensor")
@@ -65,6 +69,16 @@
     def peer(i):
         return (p, lax.rem(t + i, T), d)
 
+    z = t // 2
+    side = t % 2
+    other = 1 - side
+
+    def above(i):
+        return lax.rem(z + i, Z)
+
+    def column(i):
+        return (p, 2 * above(i) + side, d)
+
     def replica(i):
         return (p, t, lax.rem(d + i, DP))
 
@@ -88,23 +102,23 @@
 
     @pl.when(p > 0)
     def _():
-        for i in range(T):
-            pl.semaphore_signal(barrier, inc=1, device_id=(p - 1, i, d), device_id_type=MESH)
+        for i in range(2):
+            pl.semaphore_signal(barrier, inc=1, device_id=(p - 1, 2 * z + i, d), device_id_type=MESH)
 
     @pl.when(p < 3)
     def _():
-        for i in range(T):
-            pl.semaphore_signal(barrier, inc=1, device_id=(p + 1, i, d), device_id_type=MESH)
+        for i in range(2):
+            pl.semaphore_signal(barrier, inc=1, device_id=(p + 1, 2 * z + i, d), device_id_type=MESH)
 
     middle = jnp.logical_and(p > 0, p < 3)
 
     @pl.when(middle)
     def _():
-        pl.semaphore_wait(barrier, T - 1 + DP - 1 + 2 * T)
+        pl.semaphore_wait(barrier, T - 1 + DP - 1 + 4)
 
     @pl.when(jnp.logical_not(middle))
     def _():
-        pl.semaphore_wait(barrier, T - 1 + DP - 1 + T)
+        pl.semaphore_wait(barrier, T - 1 + DP - 1 + 2)
 
     def cot_copy(s, i):
         return remote(cbuf.at[s], crecv.at[s, t], cs_s.at[s, i - 1], cs_r.at[s, i - 1], peer(i))
@@ -113,18 +127,24 @@
         src = lax.rem(t + T - i, T)
         return remote(cbuf.at[s], crecv.at[s, src], cs_s.at[s, i - 1], cs_r.at[s, i - 1], peer(i))
 
-    @pl.when(first)
-    def _():
-        for s in range(S):
+    def cot_send(s):
+        @pl.when(first)
+        def _():
             cbuf[s] = cot_ref[s]
             for i in range(1, T):
                 cot_copy(s, i).start()
             crecv[s, t] = cot_ref[s]
 
+    cot_send(0)
+
     rr = iota((L, L), 0)
     tt = iota((L, L), 1)
-    lower = (rr >= tt).astype(F32)
     upper = (rr <= tt).astype(F32)
+    eye = (iota((HEADS, HEADS), 0) == iota((HEADS, HEADS), 1)).astype(F32)
+
+    def upright(row):
+        return jnp.sum(eye * row, axis=1, keepdims=True)
+
     rate = -jnp.exp(al_ref[...])
     spread = (iota((HEADS, X), 0) == iota((HEADS, X), 1) // 64).astype(F32)
     skl[...] = dot(sk_ref[...], spread, NN, HIGH)
@@ -143,12 +163,13 @@
             abf[s, :, at] = (c * sig).astype(BF16)
 
         loop(C // 128, conv)
-        z = dtr_ref[s] + db_ref[...]
-        dt = jnp.maximum(z, 0.0) + jnp.log1p(jnp.exp(-jnp.abs(z)))
-        dtc[s] = dt
-        dta = dt * rate
-        scol[...] = dot(lower, dta, NN, HIGH)
-        sT[...] = dot(dta, upper, TN, HIGH)
+        raw = dtr_ref[s] + upright(db_ref[...])
+        dt = jnp.maximum(raw, 0.0) + jnp.log1p(jnp.exp(-jnp.abs(raw)))
+        total = dot(dt * upright(rate), upper, NN, HIGH)
+        sT[...] = total
+        scol[...] = dot(total, eye, TN, HIGH)
+        dtc[s] = dot(dt, eye, TN, HIGH)
+        sgc[s] = dot(1.0 / (1.0 + jnp.exp(-raw)), eye, TN, HIGH)
         dcb[...] = dot(abf[s, :, X : X + N], abf[s, :, X + N : X + 2 * N], NT)
 
         def pair(j):
@@ -181,27 +202,60 @@
         return remote(yb.at[src, s], yb.at[src, s], yb_s.at[s, i - 1], yb_r.at[s, i - 1], replica(i))
 
     local(u_hbm, u_ref, 0).wait()
+    forward(0)
+    cot_send(1)
+    forward(1)
     for s in range(S):
-        forward(s)
         for i in range(1, DP):
             yb_copy(s, i).start()
 
     local(wout_hbm, wout, 1).wait()
-    local(win_hbm, win, 2).wait()
-
-    def g_arrival(s, k):
-        return remote(gbuf.at[s, k], gbuf.at[s, k], g_s.at[s, 0], g_r.at[s, k], peer(1))
+
+    def b_copy(s, q, to):
+        return remote(
+            psum.at[s, q], pbuf.at[s, q, side], b_s.at[s, q, to], b_r.at[s, q, side],
+            (p - 1, 2 * z + to, d),
+        )
+
+    def b_arrival(s, q, src):
+        return remote(
+            psum.at[s, q], pbuf.at[s, q, src], b_s.at[s, q, src], b_r.at[s, q, src],
+            (p + 1, 2 * z + src, d),
+        )
+
+    def c_copy(s, q, i):
+        at = gbuf.at[s, Q * z + q]
+        return remote(at, at, c_s.at[s, q, i - 1], c_r.at[s, q, i - 1], column(i))
+
+    def c_arrival(s, q, i):
+        at = gbuf.at[s, Q * above(Z - i) + q]
+        return remote(at, at, c_s.at[s, q, i - 1], c_r.at[s, q, i - 1], column(i))
+
+    def gather(s, q):
+        @pl.when(p < 3)
+        def _():
+            for src in range(2):
+                b_arrival(s, q, src).wait_recv()
+
+            def block(j):
+                at = lanes(j)
+                total = pbuf[s, q, 0, :, at].astype(F32) + pbuf[s, q, 1, :, at].astype(F32)
+                gbuf[s, Q * z + q, :, at] = total.astype(BF16)
+
+            loop(W // 128, block)
+            for i in (2, 1, 3):
+                c_copy(s, q, i).start()
 
     def gx_copy(s, i):
         to = lax.rem(d + i, DP)
         return remote(
-            gbuf.at[s, pl.ds(2 * to, 2)], gcols.at[d, s], gx_s.at[s, i - 1], gx_r.at[s, i - 1], replica(i)
+            gbuf.at[s, pl.ds(Q * to, Q)], gcols.at[d, s], gx_s.at[s, i - 1], gx_r.at[s, i - 1], replica(i)
         )
 
     def gx_arrival(s, i):
         src = lax.rem(d + DP - i, DP)
         return remote(
-            gbuf.at[s, pl.ds(0, 2)], gcols.at[src, s], gx_s.at[s, i - 1], gx_r.at[s, i - 1], replica(i)
+            gbuf.at[s, pl.ds(0, Q)], gcols.at[src, s], gx_s.at[s, i - 1], gx_r.at[s, i - 1], replica(i)
         )
 
     def grad_mix(s):
@@ -214,24 +268,43 @@
                 rows = crecv[s, :, :, lanes(k, W)].astype(F32)
                 gbuf[s, k] = rows.reshape(L, W).astype(BF16)
 
-            loop(T, block)
-
-        dyacc[...] = jnp.zeros_like(dyacc)
-
-        def block(i):
-            k = lax.rem(t + i, T)
+            loop(B, block)
+
+        for q in range(Q):
 
             @pl.when(p < 3)
             def _():
-                g_arrival(s, k).wait_recv()
-
-            dyacc[...] += dot(gbuf[s, k], wout[:, lanes(k, W)], NT)
-
-        loop(T, block)
-        dybf[...] = dyacc[...].astype(BF16)
+                for i in range(1, Z):
+                    c_arrival(s, q, i).wait_recv()
+
+            part = None
+            for i in range(Z):
+                k = Q * above(Z - i) + q
+                term = dot(gbuf[s, k], wout[:, lanes(k, W)], NT)
+                part = term if part is None else part + term
+            if q == 0:
+                dyacc[...] = part
+            elif q < Q - 1:
+                dyacc[...] += part
+            else:
+                dybf[...] = (dyacc[...] + part).astype(BF16)
         for i in range(1, DP):
             gx_copy(s, i).start()
-        gcols[d, s] = gbuf[s, pl.ds(2 * d, 2)]
+        gcols[d, s] = gbuf[s, pl.ds(Q * d, Q)]
+
+    def o_copy(s):
+        return remote(orow.at[s], gi_v.at[s], o_s.at[s], o_r.at[s], (p + 1, t, d))
+
+    def share(s):
+        @pl.when(p < 3)
+        def _():
+            for k in range(B):
+                rows = gbuf[s, k].astype(F32).reshape(T, R, W)
+                mine = jnp.where(t == 0, rows[0], 0.0)
+                for i in range(1, T):
+                    mine = jnp.where(t == i, rows[i], mine)
+                orow[s, :, k * W : (k + 1) * W] = mine.astype(BF16)
+            o_copy(s).start()
 
     def pull(s):
         dcb[...] = jnp.zeros_like(dcb)
@@ -262,53 +335,54 @@
 
         loop(C // 128, conv)
 
-    def rs_copy(s, j):
-        return remote(sbuf.at[j], rbuf.at[s, j], rs_s.at[s, j], rs_r.at[s, j], peer(1 + j))
+    def a_copy(s, q, i):
+        return remote(sbuf.at[q, i - 1], rbuf.at[s, q, i - 1], a_s.at[s, q, i - 1], a_r.at[s, q, i - 1], column(i))
 
     def scatter(s):
-        def block(j):
-            k = lax.rem(t + 1 + j, T)
-            part = dot(dubf[...], win[lanes(k, W), :], NT)
-            sbuf[j] = part.astype(BF16)
-            rs_copy(s, j).start()
-
-        loop(T - 1, block)
-        own[...] = dot(dubf[...], win[lanes(t, W), :], NT)
-
-    def g_copy(s, i):
-        return remote(opart.at[s], gbuf.at[s, t], g_s.at[s, i], g_r.at[s, t], (p - 1, i, d))
-
-    def ox_copy(s, i):
-        return remote(
-            obuf.at[s, lax.rem(t + i, T)], girecv.at[s, t], ox_s.at[s, i - 1], ox_r.at[s, i - 1], peer(i)
-        )
-
-    def ox_arrival(s, i):
-        src = lax.rem(t + T - i, T)
-        return remote(obuf.at[s, src], girecv.at[s, src], ox_s.at[s, i - 1], ox_r.at[s, i - 1], peer(i))
-
-    def reduce(s):
-        loop(T - 1, lambda j: rs_copy(s, j).wait_recv())
-
-        def block(j):
-            at = lanes(j)
-            total = own[:, at] + gbuf[s, t, :, at].astype(F32)
-            for i in range(T - 1):
-                total = total + rbuf[s, i, :, at].astype(F32)
-            opart[s, :, at] = total.astype(BF16)
-            obuf[s, :, :, at] = total.reshape(T, R, 128).astype(BF16)
-
-        loop(W // 128, block)
+        for q in range(Q):
+            for i in (2, 1, 3, 0):
+                part = dot(dubf[...], win[lanes(Q * above(i) + q, W), :], NT)
+                if i:
+                    sbuf[q, i - 1] = part.astype(BF16)
+                    a_copy(s, q, i).start()
+                else:
+                    own[q] = part
+
+    def f_copy(s, i):
+        return remote(obuf.at[s, lax.rem(t + i, T)], grecv.at[s, t], f_s.at[s, i - 1], f_r.at[s, i - 1], peer(i))
+
+    def f_arrival(s, i):
+        at = grecv.at[s, lax.rem(t + T - i, T)]
+        return remote(obuf.at[s, t], at, f_s.at[s, i - 1], f_r.at[s, i - 1], peer(i))
+
+    def combine(s, q):
+        for i in range(1, Z):
+            a_copy(s, q, i).wait_recv()
+
+        for j in range(W // 128):
+            at = slice(j * 128, (j + 1) * 128)
+            mine = side == q // (Q // 2)
+            total = own[q, :, at] + jnp.where(mine, gbuf[s, Q * z + q, :, at].astype(F32), 0.0)
+            for i in range(Z - 1):
+                total = total + rbuf[s, q, i, :, at].astype(F32)
+            psum[s, q, :, at] = total.astype(BF16)
+
+            @pl.when(last)
+            def _():
+                obuf[s, :, q, :, at] = total.reshape(T, R, 128).astype(BF16)
 
         @pl.when(p > 0)
         def _():
-            for i in range(T):
-                g_copy(s, i).start()
-
+            for to in range(2):
+                b_copy(s, q, to).start()
+
+        for i in range(1, Z):
+            a_copy(s, q, i).wait_send()
+
+    def rows_out(s):
         for i in range(1, T):
-            ox_copy(s, i).start()
-        girecv[s, t] = obuf[s, t]
-        loop(T - 1, lambda j: rs_copy(s, j).wait_send())
+            f_copy(s, i).start()
+        grecv[s, t] = obuf[s, t]
 
     def parameters(s):
         def two(value):
@@ -338,9 +412,8 @@
         d_s, d_t, d_k = lax.fori_loop(0, PAIRS, pair, (zero, zero, jnp.zeros((8, HEADS), F32)))
         later = dot((iota((L, L), 0) <= iota((L, L), 1)).astype(F32), d_s, NN, HIGH)
         dt = dtc[s]
-        z = dtr_ref[s] + db_ref[...]
         g_al = jnp.sum(later * dt, axis=0, keepdims=True) * rate
-        g_db = jnp.sum((d_t / dt + later * rate) / (1.0 + jnp.exp(-z)), axis=0, keepdims=True)
+        g_db = jnp.sum((d_t / dt + later * rate) * sgc[s], axis=0, keepdims=True)
         small = (g_al, g_db, d_k[0:1])
 
         def conv(j):
@@ -374,48 +447,52 @@
                 yb_arrival(s, i).wait_recv()
                 gx_arrival(s, i).wait_recv()
 
-        for q in range(2):
+        for k in range(2):
 
             def block(j):
                 rows = yb[:, :, :, lanes(j, 256)].reshape(DP * S * L, 256)
-                cols = gcols[:, :, q].reshape(DP * S * L, W)
-                win[lanes(j, 256), q * W : (q + 1) * W] = dot(rows, cols, TN).astype(BF16)
+                cols = jnp.concatenate(
+                    [gcols[:, :, 2 * k + e].reshape(DP * S * L, W) for e in range(2)], axis=1
+                )
+                win[lanes(j, 256), 2 * k * W : 2 * (k + 1) * W] = dot(rows, cols, TN).astype(BF16)
 
             loop(X // 256, block)
         local(win.at[pl.ds(0, X), pl.ds(0, X)], gow_out, 3).start()
 
     dcpad[L : L + TOP, :] = jnp.zeros((TOP, C), F32)
+    for q in range(Q):
+        gather(0, q)
     grad_mix(0)
     pull(0)
+    local(win_hbm, win, 2).wait()
     scatter(0)
+    share(0)
     parameters(0)
-
-    @pl.when(p < 3)
-    def _():
-        reduce(0)
-
+    for q in range(Q):
+        combine(0, q)
+
+    @pl.when(last)
+    def _():
+        rows_out(0)
+
+    for q in range(Q):
+        gather(1, q)
     grad_mix(1)
     pull(1)
-
-    @pl.when(first)
-    def _():
-        reduce(0)
-
     scatter(1)
+    share(1)
     parameters(1)
     pgr[d] = pg[...]
     for i in range(1, DP):
         pg_copy(i).start()
+    for q in range(Q):
+        combine(1, q)
 
     @pl.when(last)
     def _():
-        projection()
-
-    reduce(1)
-
-    @pl.when(p > 0)
-    def _():
-        projection()
+        rows_out(1)
+
+    projection()
 
     for i in range(1, DP):
         pg_arrival(i).wait_recv()
@@ -424,11 +501,21 @@
         total = total + pgr[i]
     pgsum[...] = total
     local(pgsum, pg_out, 4).start()
-    for s in range(S):
-        for i in range(1, T):
-            ox_arrival(s, i).wait_recv()
-        for k in range(T):
-            gi_v[s, :, k * W : (k + 1) * W] = girecv[s, k]
+
+    @pl.when(last)
+    def _():
+        for s in range(S):
+            for i in range(1, T):
+                f_arrival(s, i).wait_recv()
+            for k in range(B):
+                a, b = grecv[s, 2 * (k // Q), k % Q], grecv[s, 2 * (k // Q) + 1, k % Q]
+                gi_v[s, :, k * W : (k + 1) * W] = (a.astype(F32) + b.astype(F32)).astype(BF16)
+
+    @pl.when(p > 0)
+    def _():
+        for s in range(S):
+            remote(orow.at[s], gi_v.at[s], o_s.at[s], o_r.at[s], (p - 1, t, d)).wait_recv()
+
     local(gi_v, gi_out, 5).start()
 
     @pl.when(first)
@@ -437,15 +524,28 @@
             for i in range(1, T):
                 cot_copy(s, i).wait_send()
 
+    @pl.when(p < 3)
+    def _():
+        for s in range(S):
+            o_copy(s).wait_send()
+            for q in range(Q):
+                for i in range(1, Z):
+                    c_copy(s, q, i).wait_send()
+
     @pl.when(p > 0)
     def _():
         for s in range(S):
-            for i in range(T):
-                g_copy(s, i).wait_send()
+            for q in range(Q):
+                for to in range(2):
+                    b_copy(s, q, to).wait_send()
+
+    @pl.when(last)
+    def _():
+        for s in range(S):
+            for i in range(1, T):
+                f_copy(s, i).wait_send()
 
     for s in range(S):
-        for i in range(1, T):
-            ox_copy(s, i).wait_send()
         for i in range(1, DP):
             yb_copy(s, i).wait_send()
             gx_copy(s, i).wait_send()
@@ -454,6 +554,20 @@
     local(win.at[pl.ds(0, X), pl.ds(0, X)], gow_out, 3).wait()
     local(pgsum, pg_out, 4).wait()
     local(gi_v, gi_out, 5).wait()
+
+
+def finish(gi_ref, gow_ref, pg_ref, gi, gow, cw, cb, al, db, sk):
+    gi[...] = gi_ref[...]
+
+    def rows(j):
+        gow[lanes(j, 64), :] = gow_ref[lanes(j, 64), :]
+
+    loop(X // 64, rows)
+    cw[...] = pg_ref[0:4, :]
+    cb[...] = pg_ref[4:5, :]
+    al[...] = pg_ref[5:6, 0:HEADS]
+    db[...] = pg_ref[6:7, 0:HEADS]
+    sk[...] = pg_ref[7:8, 0:HEADS]
 
 
 def shards(cot, saved_u, dt_raw, in_weight, out_weight, conv_weight, conv_bias, a_log, dt_bias, d_skip):
@@ -475,32 +589,37 @@
         pltpu.VMEM((HEADS, L), F32),
         pltpu.VMEM((L, HEADS), F32),
         pltpu.VMEM((S, L, HEADS), F32),
+        pltpu.VMEM((S, L, HEADS), F32),
         pltpu.VMEM((1, X), F32),
         pltpu.VMEM((S, R, D), BF16),
         pltpu.VMEM((S, T, R, D), BF16),
-        pltpu.VMEM((S, T, L, W), BF16),
-        pltpu.VMEM((DP, S, 2, L, W), BF16),
+        pltpu.VMEM((S, B, L, W), BF16),
+        pltpu.VMEM((DP, S, Q, L, W), BF16),
         pltpu.VMEM((L, X), F32),
         pltpu.VMEM((L, X), BF16),
         pltpu.VMEM((L, X), F32),
         pltpu.VMEM((L, L), F32),
         pltpu.VMEM((L + TOP, C), F32),
         pltpu.VMEM((L, C), BF16),
-        pltpu.VMEM((L, W), F32),
-        pltpu.VMEM((T - 1, L, W), BF16),
-        pltpu.VMEM((S, T - 1, L, W), BF16),
-        pltpu.VMEM((S, L, W), BF16),
-        pltpu.VMEM((S, T, R, W), BF16),
-        pltpu.VMEM((S, T, R, W), BF16),
+        pltpu.VMEM((Q, L, W), F32),
+        pltpu.VMEM((Q, Z - 1, L, W), BF16),
+        pltpu.VMEM((S, Q, Z - 1, L, W), BF16),
+        pltpu.VMEM((S, Q, L, W), BF16),
+        pltpu.VMEM((S, Q, 2, L, W), BF16),
+        pltpu.VMEM((S, R, D), BF16),
+        pltpu.VMEM((S, T, Q, R, W), BF16),
+        pltpu.VMEM((S, T, Q, R, W), BF16),
         pltpu.VMEM((S, R, D), BF16),
         pltpu.VMEM((8, C), F32),
         pltpu.VMEM((DP, 8, C), F32),
         pltpu.VMEM((8, C), F32),
         sem((6,)),
         sem((S, T - 1)), sem((S, T - 1)),
-        sem((S, T)), sem((S, T)),
+        sem((S, Q, Z - 1)), sem((S, Q, Z - 1)),
+        sem((S, Q, 2)), sem((S, Q, 2)),
+        sem((S, Q, Z - 1)), sem((S, Q, Z - 1)),
         sem((S, T - 1)), sem((S, T - 1)),
-        sem((S, T - 1)), sem((S, T - 1)),
+        sem((S,)), sem((S,)),
         sem((S, DP - 1)), sem((S, DP - 1)),
         sem((S, DP - 1)), sem((S, DP - 1)),
         sem((DP - 1,)), sem((DP - 1,)),
@@ -519,16 +638,25 @@
             collective_id=0, has_side_effects=True, vmem_limit_bytes=64 * 2**20 - 2**16
         ),
         name="mixer_backward",
-    )(cot, saved_u[0], in_weight[0], out_weight[0], dt_raw[0], conv_weight[0], conv_bias, a_log, dt_bias, d_skip)
-    return (
-        gi[None],
-        gow[None],
-        pg[None, 0:4],
-        pg[4:5],
-        pg[5:6, :HEADS],
-        pg[6:7, :HEADS],
-        pg[7:8, :HEADS],
-    )
+    )(cot, saved_u[0], in_weight[0], out_weight[0], jnp.swapaxes(dt_raw[0], 1, 2), conv_weight[0], conv_bias, a_log, dt_bias, d_skip)
+    outs = pl.pallas_call(
+        finish,
+        out_shape=(
+            jax.ShapeDtypeStruct((S, R, D), BF16),
+            jax.ShapeDtypeStruct((X, X), BF16),
+            jax.ShapeDtypeStruct((4, C), F32),
+            jax.ShapeDtypeStruct((1, C), F32),
+            jax.ShapeDtypeStruct((1, HEADS), F32),
+            jax.ShapeDtypeStruct((1, HEADS), F32),
+            jax.ShapeDtypeStruct((1, HEADS), F32),
+        ),
+        in_specs=[vmem_spec] * 3,
+        out_specs=(vmem_spec,) * 7,
+        compiler_params=pltpu.CompilerParams(vmem_limit_bytes=16 * 2**20),
+        name="finish",
+    )(gi, gow, pg)
+    gi, gow, cw, cb, al, db, sk = outs
+    return gi[None], gow[None], cw[None], cb, al, db, sk
 
 
 def solution(mesh):

time: 224 us -> 191 us (0.85)
  Pallas kernels: 210 us -> 186 us
  local copies, waits for them, and re-layouts: 10.5 us -> 3.38 us
    pallas_call x1, Pallas kernels: 210 us -> 184 us  [shards(): pl.pallas_call(kernel, out_shape=(jax.ShapeDtypeStruct((S, R, D), BF16),...]
    unnamed x3 -> x6, local copies, waits for them, and re-layouts: 6.4 us -> 3.38 us
    slice x2 -> x0, local copies, waits for them, and re-layouts: 2.7 us -> none  [the longest x1 1.4 us: shards(): pg[4:5]]
where the time goes in v2:
time: 191 us; the launch traced here: 190 us
  Pallas kernels  186 us (97%)
  local copies, waits for them, and re-layouts  3.38 us (2%)
    pallas_call x1, Pallas kernels, shards(): pl.pallas_call(kernel, out_shape=(jax.ShapeDtypeStruct((S, R, D), BF16),...  184 us

profile of v2, /device:TPU:0, one launch (start us, length us, event | category | flops | bytes accessed | tf_op | source)
XLA Modules:
  0.0 190.1 jit_solution(18027585597607419032)
XLA Ops:
  0.6 184.4 %mixer_backward.1 = (bf16[2,24,4096]{2,1,0:T(8,128)(2,1)}, bf16[1024,1024]{1,0:T(8,128)(2,1)}, f32[8,1536]{1,0:T(8,128)}) custom-call(bf16[2,24,4096]{2,1,0:T(8,128)(2,1)} %cot_ref.1, bf16[2,192,1536]{2,1,0:T(8,128)(2,1)} %bitcast.12, bf16[4096,1536]{1,0:T(8,128)(2,1)} %bitcast.10, bf16[1024,4096]{1,0:T(8,128)(2,1)} %bitcast.11, f32[2,16,192]{2,1,0:T(8,128)} %bitcast.13, ...), custom_call_target="tpu_custom_call" | custom-call | tf_op jit(solution)/shard_map/mixer_backward/pallas_call | solution.py:627
  185.0 0.0 copy-start
  185.1 1.6 copy-done
  186.6 0.0 copy-start.1
  186.6 1.0 copy-done.1
  187.6 0.0 copy-start.2
  187.6 0.8 copy-done.2
  188.4 1.7 finish.1
Async XLA Ops:
  185.0 1.6 copy-start
  186.6 1.0 copy-start.1
  187.6 0.8 copy-start.2

commit v3 on v2

--- a/solution.py
+++ b/solution.py
@@ -55,8 +55,8 @@
     cot_ref, u_hbm, win_hbm, wout_hbm, dtr_ref, cw_ref, cb_ref, al_ref, db_ref, sk_ref,
     gi_out, gow_out, pg_out,
     win, wout, u_ref, upad, sp, abf, xst, mt, est, y0, yb, sT, scol, dtc, sgc, skl,
-    cbuf, crecv, gbuf, gcols, dyacc, dybf, dx0, dcb, dcpad, dubf, own,
-    sbuf, rbuf, psum, pbuf, orow, obuf, grecv, gi_v, pg, pgr, pgsum,
+    cbuf, crecv, gbuf, gcols, dyacc, dybf, dx0, dcb, dcpad, own,
+    sbuf, rbuf, psum, pbuf, orow, obuf, gi_v, pg, pgr, pgsum,
     loc, cs_s, cs_r, a_s, a_r, b_s, b_r, c_s, c_r, f_s, f_r, o_s, o_r,
     yb_s, yb_r, gx_s, gx_r, pg_s, pg_r,
 ):
@@ -91,6 +91,7 @@
         )
 
     local(u_hbm, u_ref, 0).start()
+    local(cot_ref, cbuf, 6).start()
     local(wout_hbm, wout, 1).start()
     local(win_hbm, win, 2).start()
 
@@ -130,11 +131,11 @@
     def cot_send(s):
         @pl.when(first)
         def _():
-            cbuf[s] = cot_ref[s]
             for i in range(1, T):
                 cot_copy(s, i).start()
-            crecv[s, t] = cot_ref[s]
-
+            crecv[s, t] = cbuf[s]
+
+    local(cot_ref, cbuf, 6).wait()
     cot_send(0)
 
     rr = iota((L, L), 0)
@@ -287,7 +288,7 @@
             elif q < Q - 1:
                 dyacc[...] += part
             else:
-                dybf[...] = (dyacc[...] + part).astype(BF16)
+                dybf[s] = (dyacc[...] + part).astype(BF16)
         for i in range(1, DP):
             gx_copy(s, i).start()
         gcols[d, s] = gbuf[s, pl.ds(Q * d, Q)]
@@ -311,27 +312,27 @@
 
         def pair(j):
             at = lanes(j)
-            dy2 = dybf[:, at]
+            dy2 = dybf[s, :, at]
             dm = dot(xst[s, j], dy2, NT)
             dcb[...] += dm[:L] * est[s, j, 0:L, :].astype(F32) + dm[L:] * est[s, j, L : 2 * L, :].astype(F32)
             dx = dot(mt[s, j], dy2, NN)
             dx = jnp.where(iota((L, 128), 1) < 64, dx[:L], dx[L:])
-            dx0[:, at] = dx
-            dcpad[0:L, at] = (dx + skl[:, at] * dy2.astype(F32)) * sp[s, :, at]
+            dx0[s, :, at] = dx
+            dcpad[s, 0:L, at] = (dx + skl[:, at] * dy2.astype(F32)) * sp[s, :, at]
 
         loop(PAIRS, pair)
         low = dcb[...].astype(BF16)
-        dcpad[0:L, X : X + N] = dot(low, abf[s, :, X + N : X + 2 * N], NN) * sp[s, :, X : X + N]
-        dcpad[0:L, X + N : X + 2 * N] = (
+        dcpad[s, 0:L, X : X + N] = dot(low, abf[s, :, X + N : X + 2 * N], NN) * sp[s, :, X : X + N]
+        dcpad[s, 0:L, X + N : X + 2 * N] = (
             dot(low, abf[s, :, X : X + N], TN) * sp[s, :, X + N : X + 2 * N]
         )
 
         def conv(j):
             at = lanes(j)
-            du = cw_ref[3:4, at] * dcpad[0:L, at]
+            du = cw_ref[3:4, at] * dcpad[s, 0:L, at]
             for k in range(3):
-                du = du + cw_ref[k : k + 1, at] * dcpad[3 - k : 3 - k + L, at]
-            dubf[:, at] = du.astype(BF16)
+                du = du + cw_ref[k : k + 1, at] * dcpad[s, 3 - k : 3 - k + L, at]
+            u_ref[0, :, at] = du.astype(BF16)
 
         loop(C // 128, conv)
 
@@ -341,7 +342,7 @@
     def scatter(s):
         for q in range(Q):
             for i in (2, 1, 3, 0):
-                part = dot(dubf[...], win[lanes(Q * above(i) + q, W), :], NT)
+                part = dot(u_ref[0], win[lanes(Q * above(i) + q, W), :], NT)
                 if i:
                     sbuf[q, i - 1] = part.astype(BF16)
                     a_copy(s, q, i).start()
@@ -349,10 +350,10 @@
                     own[q] = part
 
     def f_copy(s, i):
-        return remote(obuf.at[s, lax.rem(t + i, T)], grecv.at[s, t], f_s.at[s, i - 1], f_r.at[s, i - 1], peer(i))
+        return remote(obuf.at[s, lax.rem(t + i, T)], crecv.at[s, t, :, pl.ds(0, Q * W)], f_s.at[s, i - 1], f_r.at[s, i - 1], peer(i))
 
     def f_arrival(s, i):
-        at = grecv.at[s, lax.rem(t + T - i, T)]
+        at = crecv.at[s, lax.rem(t + T - i, T), :, pl.ds(0, Q * W)]
         return remote(obuf.at[s, t], at, f_s.at[s, i - 1], f_r.at[s, i - 1], peer(i))
 
     def combine(s, q):
@@ -369,7 +370,7 @@
 
             @pl.when(last)
             def _():
-                obuf[s, :, q, :, at] = total.reshape(T, R, 128).astype(BF16)
+                obuf[s, :, :, q * W + j * 128 : q * W + (j + 1) * 128] = total.reshape(T, R, 128).astype(BF16)
 
         @pl.when(p > 0)
         def _():
@@ -382,7 +383,7 @@
     def rows_out(s):
         for i in range(1, T):
             f_copy(s, i).start()
-        grecv[s, t] = obuf[s, t]
+        crecv[s, t, :, 0 : Q * W] = obuf[s, t]
 
     def parameters(s):
         def two(value):
@@ -393,9 +394,9 @@
         def pair(j, carry):
             d_s, d_t, d_k = carry
             at = lanes(j)
-            dy2 = dybf[:, at].astype(F32)
+            dy2 = dybf[s, :, at].astype(F32)
             x2 = abf[s, :, at].astype(F32)
-            inner = x2 * dx0[:, at]
+            inner = x2 * dx0[s, :, at]
             outer = dy2 * y0[s, :, at] - inner
             lane = iota((2 * 128, HEADS), 0)
             lane = jnp.where(lane >= 128, lane - 128, lane)
@@ -418,7 +419,7 @@
 
         def conv(j):
             at = lanes(j)
-            dc = dcpad[0:L, at]
+            dc = dcpad[s, 0:L, at]
             rows = []
             for k in range(4):
                 rows.append(jnp.sum(dc * upad[s, TOP - 3 + k : TOP - 3 + k + L, at], axis=0, keepdims=True))
@@ -459,15 +460,15 @@
             loop(X // 256, block)
         local(win.at[pl.ds(0, X), pl.ds(0, X)], gow_out, 3).start()
 
-    dcpad[L : L + TOP, :] = jnp.zeros((TOP, C), F32)
+    dcpad[:, L : L + TOP, :] = jnp.zeros((S, TOP, C), F32)
     for q in range(Q):
         gather(0, q)
     grad_mix(0)
     pull(0)
     local(win_hbm, win, 2).wait()
     scatter(0)
-    share(0)
-    parameters(0)
+    for q in range(Q):
+        gather(1, q)
     for q in range(Q):
         combine(0, q)
 
@@ -475,23 +476,32 @@
     def _():
         rows_out(0)
 
-    for q in range(Q):
-        gather(1, q)
+
+    @pl.when(p < 3)
+    def _():
+        share(0)
+        parameters(0)
+
     grad_mix(1)
     pull(1)
     scatter(1)
+
+    @pl.when(first)
+    def _():
+        parameters(0)
+
+    for q in range(Q):
+        combine(1, q)
+
+    @pl.when(last)
+    def _():
+        rows_out(1)
+
     share(1)
     parameters(1)
     pgr[d] = pg[...]
     for i in range(1, DP):
         pg_copy(i).start()
-    for q in range(Q):
-        combine(1, q)
-
-    @pl.when(last)
-    def _():
-        rows_out(1)
-
     projection()
 
     for i in range(1, DP):
@@ -507,9 +517,9 @@
         for s in range(S):
             for i in range(1, T):
                 f_arrival(s, i).wait_recv()
-            for k in range(B):
-                a, b = grecv[s, 2 * (k // Q), k % Q], grecv[s, 2 * (k // Q) + 1, k % Q]
-                gi_v[s, :, k * W : (k + 1) * W] = (a.astype(F32) + b.astype(F32)).astype(BF16)
+            for k in range(Z):
+                a, b = crecv[s, 2 * k, :, 0 : Q * W], crecv[s, 2 * k + 1, :, 0 : Q * W]
+                gi_v[s, :, k * Q * W : (k + 1) * Q * W] = (a.astype(F32) + b.astype(F32)).astype(BF16)
 
     @pl.when(p > 0)
     def _():
@@ -556,18 +566,21 @@
     local(gi_v, gi_out, 5).wait()
 
 
-def finish(gi_ref, gow_ref, pg_ref, gi, gow, cw, cb, al, db, sk):
-    gi[...] = gi_ref[...]
-
-    def rows(j):
-        gow[lanes(j, 64), :] = gow_ref[lanes(j, 64), :]
-
-    loop(X // 64, rows)
-    cw[...] = pg_ref[0:4, :]
-    cb[...] = pg_ref[4:5, :]
-    al[...] = pg_ref[5:6, 0:HEADS]
-    db[...] = pg_ref[6:7, 0:HEADS]
-    sk[...] = pg_ref[7:8, 0:HEADS]
+def finish(gi_ref, gow_ref, pg_ref, gi, gow, cw, cb, al, db, sk, pg, sems):
+    copies = [
+        pltpu.make_async_copy(src, dst, sems.at[i])
+        for i, (src, dst) in enumerate(((gow_ref, gow), (gi_ref, gi), (pg_ref, pg)))
+    ]
+    for copy in copies:
+        copy.start()
+    copies[2].wait()
+    cw[...] = pg[0:4, :]
+    cb[...] = pg[4:5, :]
+    al[...] = pg[5:6, 0:HEADS]
+    db[...] = pg[6:7, 0:HEADS]
+    sk[...] = pg[7:8, 0:HEADS]
+    copies[1].wait()
+    copies[0].wait()
 
 
 def shards(cot, saved_u, dt_raw, in_weight, out_weight, conv_weight, conv_bias, a_log, dt_bias, d_skip):
@@ -596,24 +609,22 @@
         pltpu.VMEM((S, B, L, W), BF16),
         pltpu.VMEM((DP, S, Q, L, W), BF16),
         pltpu.VMEM((L, X), F32),
-        pltpu.VMEM((L, X), BF16),
-        pltpu.VMEM((L, X), F32),
+        pltpu.VMEM((S, L, X), BF16),
+        pltpu.VMEM((S, L, X), F32),
         pltpu.VMEM((L, L), F32),
-        pltpu.VMEM((L + TOP, C), F32),
-        pltpu.VMEM((L, C), BF16),
+        pltpu.VMEM((S, L + TOP, C), F32),
         pltpu.VMEM((Q, L, W), F32),
         pltpu.VMEM((Q, Z - 1, L, W), BF16),
         pltpu.VMEM((S, Q, Z - 1, L, W), BF16),
         pltpu.VMEM((S, Q, L, W), BF16),
         pltpu.VMEM((S, Q, 2, L, W), BF16),
         pltpu.VMEM((S, R, D), BF16),
-        pltpu.VMEM((S, T, Q, R, W), BF16),
-        pltpu.VMEM((S, T, Q, R, W), BF16),
+        pltpu.VMEM((S, T, R, Q * W), BF16),
         pltpu.VMEM((S, R, D), BF16),
         pltpu.VMEM((8, C), F32),
         pltpu.VMEM((DP, 8, C), F32),
         pltpu.VMEM((8, C), F32),
-        sem((6,)),
+        sem((7,)),
         sem((S, T - 1)), sem((S, T - 1)),
         sem((S, Q, Z - 1)), sem((S, Q, Z - 1)),
         sem((S, Q, 2)), sem((S, Q, 2)),
@@ -631,7 +642,7 @@
             jax.ShapeDtypeStruct((X, X), BF16),
             jax.ShapeDtypeStruct((8, C), F32),
         ),
-        in_specs=[vmem_spec, any_spec, any_spec, any_spec] + [vmem_spec] * 6,
+        in_specs=[any_spec, any_spec, any_spec, any_spec] + [vmem_spec] * 6,
         out_specs=(any_spec, any_spec, any_spec),
         scratch_shapes=scratch,
         compiler_params=pltpu.CompilerParams(
@@ -650,9 +661,10 @@
             jax.ShapeDtypeStruct((1, HEADS), F32),
             jax.ShapeDtypeStruct((1, HEADS), F32),
         ),
-        in_specs=[vmem_spec] * 3,
+        in_specs=[any_spec] * 3,
         out_specs=(vmem_spec,) * 7,
-        compiler_params=pltpu.CompilerParams(vmem_limit_bytes=16 * 2**20),
+        scratch_shapes=[pltpu.VMEM((8, C), F32), sem((3,))],
+        compiler_params=pltpu.CompilerParams(vmem_limit_bytes=64 * 2**20 - 2**16),
         name="finish",
     )(gi, gow, pg)
     gi, gow, cw, cb, al, db, sk = outs

time: 191 us -> 171 us (0.90)
  Pallas kernels: 186 us -> 170 us
  local copies, waits for them, and re-layouts: 3.38 us -> 0 us
    pallas_call x1, Pallas kernels: 184 us -> 167 us  [shards(): pl.pallas_call(kernel, out_shape=(jax.ShapeDtypeStruct((S, R, D), BF16),...]
    unnamed x6 -> x0, local copies, waits for them, and re-layouts: 3.38 us -> none
where the time goes in v3:
time: 171 us
  Pallas kernels  170 us (99%)
    pallas_call x1, Pallas kernels, shards(): pl.pallas_call(kernel, out_shape=(jax.ShapeDtypeStruct((S, R, D), BF16),...  167 us

profile of v3, /device:TPU:0, one launch (start us, length us, event | category | flops | bytes accessed | tf_op | source)
XLA Modules:
  0.0 170.9 jit_solution(5878960753514269265)
XLA Ops:
  0.6 167.0 %mixer_backward.1 = (bf16[2,24,4096]{2,1,0:T(8,128)(2,1)}, bf16[1024,1024]{1,0:T(8,128)(2,1)}, f32[8,1536]{1,0:T(8,128)}) custom-call(bf16[2,24,4096]{2,1,0:T(8,128)(2,1)} %cot_ref.1, bf16[2,192,1536]{2,1,0:T(8,128)(2,1)} %bitcast.12, bf16[4096,1536]{1,0:T(8,128)(2,1)} %bitcast.10, bf16[1024,4096]{1,0:T(8,128)(2,1)} %bitcast.11, f32[2,16,192]{2,1,0:T(8,128)} %bitcast.13, ...), custom_call_target="tpu_custom_call" | custom-call | tf_op jit(solution)/shard_map/mixer_backward/pallas_call | solution.py:638
  167.6 3.1 %finish.1 = (bf16[2,24,4096]{2,1,0:T(8,128)(2,1)}, bf16[1024,1024]{1,0:T(8,128)(2,1)}, f32[4,1536]{1,0:T(4,128)}, f32[1,1536]{1,0:T(1,128)}, f32[1,16]{1,0:T(1,128)}, /*index=5*/f32[1,16]{1,0:T(1,128)}, f32[1,16]{1,0:T(1,128)}) custom-call(bf16[2,24,4096]{2,1,0:T(8,128)(2,1)} %get-tuple-element.17.gi_ref, bf16[1024,1024]{1,0:T(8,128)(2,1)} %get-tuple-element.18.gow_ref, ...), custom_call_target="tpu_custom_call" | custom-call | tf_op jit(solution)/shard_map/finish/pallas_call | solution.py:653

commit v4 on v3

--- a/solution.py
+++ b/solution.py
@@ -374,8 +374,8 @@
 
         @pl.when(p > 0)
         def _():
-            for to in range(2):
-                b_copy(s, q, to).start()
+            b_copy(s, q, other).start()
+            b_copy(s, q, side).start()
 
         for i in range(1, Z):
             a_copy(s, q, i).wait_send()
@@ -490,6 +490,17 @@
     def _():
         parameters(0)
 
+    def sum_parameters():
+        share(1)
+        parameters(1)
+        pgr[d] = pg[...]
+        for i in range(1, DP):
+            pg_copy(i).start()
+
+    @pl.when(last)
+    def _():
+        sum_parameters()
+
     for q in range(Q):
         combine(1, q)
 
@@ -497,11 +508,10 @@
     def _():
         rows_out(1)
 
-    share(1)
-    parameters(1)
-    pgr[d] = pg[...]
-    for i in range(1, DP):
-        pg_copy(i).start()
+    @pl.when(p > 0)
+    def _():
+        sum_parameters()
+
     projection()
 
     for i in range(1, DP):

time: 171 us -> 169 us (0.988)
  Pallas kernels: 170 us -> 168 us
    pallas_call x1, Pallas kernels: 167 us -> 164 us  [shards(): pl.pallas_call(kernel, out_shape=(jax.ShapeDtypeStruct((S, R, D), BF16),...]
where the time goes in v4:
time: 169 us; the launch traced here: 168 us
  Pallas kernels  168 us (99%)
    pallas_call x1, Pallas kernels, shards(): pl.pallas_call(kernel, out_shape=(jax.ShapeDtypeStruct((S, R, D), BF16),...  164 us

profile of v4, /device:TPU:0, one launch (start us, length us, event | category | flops | bytes accessed | tf_op | source)
XLA Modules:
  0.0 168.3 jit_solution(8906185104356254102)
XLA Ops:
  0.6 164.4 %mixer_backward.1 = (bf16[2,24,4096]{2,1,0:T(8,128)(2,1)}, bf16[1024,1024]{1,0:T(8,128)(2,1)}, f32[8,1536]{1,0:T(8,128)}) custom-call(bf16[2,24,4096]{2,1,0:T(8,128)(2,1)} %cot_ref.1, bf16[2,192,1536]{2,1,0:T(8,128)(2,1)} %bitcast.12, bf16[4096,1536]{1,0:T(8,128)(2,1)} %bitcast.10, bf16[1024,4096]{1,0:T(8,128)(2,1)} %bitcast.11, f32[2,16,192]{2,1,0:T(8,128)} %bitcast.13, ...), custom_call_target="tpu_custom_call" | custom-call | tf_op jit(solution)/shard_map/mixer_backward/pallas_call | solution.py:648
  165.0 3.1 %finish.1 = (bf16[2,24,4096]{2,1,0:T(8,128)(2,1)}, bf16[1024,1024]{1,0:T(8,128)(2,1)}, f32[4,1536]{1,0:T(4,128)}, f32[1,1536]{1,0:T(1,128)}, f32[1,16]{1,0:T(1,128)}, /*index=5*/f32[1,16]{1,0:T(1,128)}, f32[1,16]{1,0:T(1,128)}) custom-call(bf16[2,24,4096]{2,1,0:T(8,128)(2,1)} %get-tuple-element.17.gi_ref, bf16[1024,1024]{1,0:T(8,128)(2,1)} %get-tuple-element.18.gow_ref, ...), custom_call_target="tpu_custom_call" | custom-call | tf_op jit(solution)/shard_map/finish/pallas_call | solution.py:663

commit v5 on v4

--- a/solution.py
+++ b/solution.py
@@ -349,6 +349,11 @@
                 else:
                     own[q] = part
 
+    def sent(s):
+        for q in range(Q):
+            for i in range(1, Z):
+                a_copy(s, q, i).wait_send()
+
     def f_copy(s, i):
         return remote(obuf.at[s, lax.rem(t + i, T)], crecv.at[s, t, :, pl.ds(0, Q * W)], f_s.at[s, i - 1], f_r.at[s, i - 1], peer(i))
 
@@ -377,8 +382,6 @@
             b_copy(s, q, other).start()
             b_copy(s, q, side).start()
 
-        for i in range(1, Z):
-            a_copy(s, q, i).wait_send()
 
     def rows_out(s):
         for i in range(1, T):
@@ -484,6 +487,7 @@
 
     grad_mix(1)
     pull(1)
+    sent(0)
     scatter(1)
 
     @pl.when(first)
@@ -569,6 +573,7 @@
         for i in range(1, DP):
             yb_copy(s, i).wait_send()
             gx_copy(s, i).wait_send()
+    sent(1)
     for i in range(1, DP):
         pg_copy(i).wait_send()
     local(win.at[pl.ds(0, X), pl.ds(0, X)], gow_out, 3).wait()

time: 169 us -> 169 us (level)
  no operation moved by 1% of the time
where the time goes in v5:
time: 169 us; the launch traced here: 168 us
  Pallas kernels  167 us (99%)
    pallas_call x1, Pallas kernels, shards(): pl.pallas_call(kernel, out_shape=(jax.ShapeDtypeStruct((S, R, D), BF16),...  164 us

profile of v5, /device:TPU:0, one launch (start us, length us, event | category | flops | bytes accessed | tf_op | source)
XLA Modules:
  0.0 168.3 jit_solution(3458162249009231409)
XLA Ops:
  0.6 164.4 %mixer_backward.1 = (bf16[2,24,4096]{2,1,0:T(8,128)(2,1)}, bf16[1024,1024]{1,0:T(8,128)(2,1)}, f32[8,1536]{1,0:T(8,128)}) custom-call(bf16[2,24,4096]{2,1,0:T(8,128)(2,1)} %cot_ref.1, bf16[2,192,1536]{2,1,0:T(8,128)(2,1)} %bitcast.12, bf16[4096,1536]{1,0:T(8,128)(2,1)} %bitcast.10, bf16[1024,4096]{1,0:T(8,128)(2,1)} %bitcast.11, f32[2,16,192]{2,1,0:T(8,128)} %bitcast.13, ...), custom_call_target="tpu_custom_call" | custom-call | tf_op jit(solution)/shard_map/mixer_backward/pallas_call | solution.py:653
  165.0 3.1 %finish.1 = (bf16[2,24,4096]{2,1,0:T(8,128)(2,1)}, bf16[1024,1024]{1,0:T(8,128)(2,1)}, f32[4,1536]{1,0:T(4,128)}, f32[1,1536]{1,0:T(1,128)}, f32[1,16]{1,0:T(1,128)}, /*index=5*/f32[1,16]{1,0:T(1,128)}, f32[1,16]{1,0:T(1,128)}) custom-call(bf16[2,24,4096]{2,1,0:T(8,128)(2,1)} %get-tuple-element.17.gi_ref, bf16[1024,1024]{1,0:T(8,128)(2,1)} %get-tuple-element.18.gow_ref, ...), custom_call_target="tpu_custom_call" | custom-call | tf_op jit(solution)/shard_map/finish/pallas_call | solution.py:668
